TPU v7x, 256 devices: a whole 4x4x8 slice. The times are simulated.
256 devices in a mesh: dp: 8 (over y, z_lo), expert: 32 (over x, z_hi, core).
Axes of the slice: x: 4, y: 4, z: 8 (z_hi: 4, z_lo: 2; z = z_hi * 2 + z_lo), core: 2. Of those that a mesh axis runs over, the one named last changes fastest.
Arguments:
- tokens: bfloat16 [8, 2048, 4096], P('dp', 'expert'), may hold values from -6 to 6, as said below
- out_grad: bfloat16 [8, 2048, 4096], P('dp', 'expert'), may hold values from -0.75 to 0.75
- router: bfloat16 [4096, 32], replicated, may hold values from -0.09375 to 0.09375
- choice_index: int32 [8, 32, 32], P('dp'), may hold values from 0 to 2047, as said below
- gate_weight: bfloat16 [32, 1536, 4096], P('expert', 'dp'), as said below
- up_weight: bfloat16 [32, 1536, 4096], P('expert', 'dp'), as said below
- down_weight: bfloat16 [32, 1536, 4096], P('expert', None, 'dp'), as said below
Outputs:
- mixed: bfloat16 [8, 2048, 4096], P('dp', 'expert')
- token_grad: bfloat16 [8, 2048, 4096], P('dp', 'expert')
- router_grad: float32 [4096, 32], replicated
- gate_grad: bfloat16 [32, 1536, 4096], P('expert', 'dp')
- up_grad: bfloat16 [32, 1536, 4096], P('expert', 'dp')
- down_grad: bfloat16 [32, 1536, 4096], P('expert', None, 'dp')
Inputs may be any that keep to these rules, and one draw needn't show every extreme that they name: `tokens`: each entry is an FP4 (E2M1) value times a power of two shared by each aligned block of 16 entries along the last dimension, times a fixed power of two. `gate_weight`: each entry is an FP4 (E2M1) value times a power of two shared by each aligned block of 16 entries along the last dimension, times a fixed power of two set by the fan-in. `up_weight`: as for gate_weight. `down_weight`: as for gate_weight. `choice_index`: each list of 32 indices names distinct tokens of its group; at most 2 of them lie among the 64 tokens of one device, and in every list some device has exactly 2.
All inputs are finite; a program needn't handle non-finite values.
Results may differ from a plain program's by a relative error of at most 0.0064.
Values may be sent and summed in bfloat16 or wider, within the bound.
No kernel may reach another device: no remote copies, remote signals or barrier semaphores. Data moves between devices by JAX's collectives and lax.ppermute only.
A program may use at most 64 MiB of HBM per device.

v0:
```python
import jax
import jax.numpy as jnp
from jax import lax
from jax.sharding import PartitionSpec as P

MOST = 2


def local(tokens, out_grad, router, choice_index, gate_weight, up_weight, down_weight):
    highest = lax.Precision.HIGHEST
    local_rows = tokens[0]
    local_grads = out_grad[0]
    tok_count = local_rows.shape[0]
    table = choice_index[0]
    cap_size = table.shape[1]
    local_experts = gate_weight.shape[0]
    source = lax.axis_index("expert")
    n_source = lax.axis_size("expert")
    logits = jnp.dot(local_rows, router, preferred_element_type=jnp.float32)
    gates = jax.nn.sigmoid(logits)
    owner_dev = table // tok_count
    offsets = table - owner_dev * tok_count
    earlier = jnp.arange(cap_size)[None, :] < jnp.arange(cap_size)[:, None]
    same_owner = owner_dev[:, :, None] == owner_dev[:, None, :]
    rank_ids = jnp.sum(same_owner & earlier[None], axis=2)
    mine = owner_dev == source
    pick_slot = (
        mine[:, :, None]
        & (rank_ids[:, :, None] == jnp.arange(MOST, dtype=jnp.int32)[None, None, :])
    ).astype(jnp.float32)
    pick_token = (
        offsets[:, :, None] == jnp.arange(tok_count, dtype=jnp.int32)[None, None, :]
    ).astype(jnp.float32)
    select = jnp.einsum("ekm,ekt->emt", pick_slot, pick_token, precision=highest)
    select_low = select.astype(jnp.bfloat16)
    slot_gate = jnp.einsum("emt,te->em", select, gates, precision=highest)
    row_slots = jnp.einsum(
        "emt,td->emd", select_low, local_rows, preferred_element_type=jnp.float32
    ).astype(jnp.bfloat16)
    grad_slots = jnp.einsum(
        "emt,td->emd", select_low, local_grads, preferred_element_type=jnp.float32
    ).astype(jnp.bfloat16)
    gated_slots = (slot_gate[:, :, None] * grad_slots.astype(jnp.float32)).astype(jnp.bfloat16)
    rows_recv, gated_recv = (
        lax.all_to_all(row_slots, "expert", split_axis=0, concat_axis=1, tiled=True),
        lax.all_to_all(gated_slots, "expert", split_axis=0, concat_axis=1, tiled=True),
    )
    first_expert = source * local_experts
    own_owner = lax.dynamic_slice_in_dim(owner_dev, first_expert, local_experts, 0)
    own_rank = lax.dynamic_slice_in_dim(rank_ids, first_expert, local_experts, 0)
    slot_ids = own_owner * MOST + own_rank
    compact = (
        slot_ids[:, :, None] == jnp.arange(n_source * MOST, dtype=jnp.int32)[None, None, :]
    ).astype(jnp.bfloat16)
    expert_rows = jnp.einsum(
        "lks,lsd->lkd", compact, rows_recv, preferred_element_type=jnp.float32
    ).astype(jnp.bfloat16)
    gated_rows = jnp.einsum(
        "lks,lsd->lkd", compact, gated_recv, preferred_element_type=jnp.float32
    ).astype(jnp.bfloat16)
    all_rows = lax.all_gather(expert_rows, "dp", axis=1, tiled=True)
    hidden_pre = jnp.einsum(
        "lrd,lfd->flr", all_rows, gate_weight, preferred_element_type=jnp.float32
    )
    up_pre = jnp.einsum("lrd,lfd->flr", all_rows, up_weight, preferred_element_type=jnp.float32)
    activated = (jax.nn.silu(hidden_pre) * up_pre).astype(jnp.bfloat16)
    act_all = lax.all_gather(activated, "dp", axis=0, tiled=True)
    out_part = jnp.einsum(
        "flr,lfc->lrc", act_all, down_weight, preferred_element_type=jnp.float32
    ).astype(jnp.bfloat16)
    out_rows = lax.all_to_all(out_part, "dp", split_axis=1, concat_axis=2, tiled=True)
    out_slots = jnp.einsum(
        "lks,lkd->lsd", compact, out_rows, preferred_element_type=jnp.float32
    ).astype(jnp.bfloat16)
    out_back = lax.all_to_all(out_slots, "expert", split_axis=1, concat_axis=0, tiled=True)
    gated_cols = lax.all_to_all(gated_rows, "dp", split_axis=2, concat_axis=1, tiled=True)
    act_diff = lax.psum_scatter(
        jnp.einsum("lrc,lfc->flr", gated_cols, down_weight, preferred_element_type=jnp.float32),
        "dp",
        scatter_dimension=0,
        tiled=True,
    )
    sigma = jax.nn.sigmoid(hidden_pre)
    hidden_diff = (act_diff * up_pre * sigma * (1.0 + hidden_pre * (1.0 - sigma))).astype(
        jnp.bfloat16
    )
    up_diff = (act_diff * hidden_pre * sigma).astype(jnp.bfloat16)
    down_grad = jnp.einsum(
        "flr,lrc->lfc", act_all, gated_cols, preferred_element_type=jnp.float32
    ).astype(jnp.bfloat16)
    gate_grad = jnp.einsum(
        "flr,lrd->lfd", hidden_diff, all_rows, preferred_element_type=jnp.float32
    ).astype(jnp.bfloat16)
    up_grad = jnp.einsum(
        "flr,lrd->lfd", up_diff, all_rows, preferred_element_type=jnp.float32
    ).astype(jnp.bfloat16)
    summed_cols = lax.psum_scatter(
        jnp.einsum("flr,lfd->dlr", hidden_diff, gate_weight, preferred_element_type=jnp.float32)
        + jnp.einsum("flr,lfd->dlr", up_diff, up_weight, preferred_element_type=jnp.float32),
        "dp",
        scatter_dimension=0,
        tiled=True,
    )
    diff_cols = summed_cols.astype(jnp.bfloat16)
    diff_back = lax.all_to_all(diff_cols, "dp", split_axis=2, concat_axis=0, tiled=True)
    diff_slots = jnp.einsum(
        "lks,dlk->lsd", compact, diff_back, preferred_element_type=jnp.float32
    ).astype(jnp.bfloat16)
    diff_recv = lax.all_to_all(diff_slots, "expert", split_axis=1, concat_axis=0, tiled=True)
    weighted = out_back.astype(jnp.float32) * slot_gate[:, :, None]
    mixed = jnp.einsum("emt,emd->td", select, weighted, precision=highest).astype(jnp.bfloat16)
    slot_dgate = jnp.sum(grad_slots.astype(jnp.float32) * out_back.astype(jnp.float32), axis=2)
    logit_diff = (
        jnp.einsum("emt,em->te", select, slot_dgate, precision=highest) * gates * (1.0 - gates)
    )
    expert_part = jnp.einsum(
        "emt,emd->td", select, diff_recv.astype(jnp.float32), precision=highest
    )
    router_part = jnp.dot(logit_diff, router.astype(jnp.float32).T, precision=highest)
    token_grad = (expert_part + router_part).astype(jnp.bfloat16)
    router_terms = jnp.dot(local_rows.astype(jnp.float32).T, logit_diff, precision=highest)
    router_grad = lax.psum(router_terms, ("dp", "expert"))
    return (mixed[None], token_grad[None], router_grad, gate_grad, up_grad, down_grad)


def solution(mesh):
    in_specs = (
        P("dp", "expert", None),
        P("dp", "expert", None),
        P(),
        P("dp", None, None),
        P("expert", "dp", None),
        P("expert", "dp", None),
        P("expert", None, "dp"),
    )
    out_specs = (
        P("dp", "expert", None),
        P("dp", "expert", None),
        P(),
        P("expert", "dp", None),
        P("expert", "dp", None),
        P("expert", None, "dp"),
    )
    return jax.shard_map(local, mesh=mesh, in_specs=in_specs, out_specs=out_specs, check_vma=False)
```

profile of v0, /device:TPU:1, one launch (start us, length us, event | category | flops | bytes accessed | tf_op | source)
XLA Modules:
  0.0 727.9 jit_solution(15045352132563692942)
XLA Ops:
  12.6 12.6 %all-to-all-start = ((bf16[32,2,4096]{2,1,0:T(2,128)(2,1)}), bf16[32,2,4096]{2,1,0:T(2,128)(2,1)S(1)}, u32[]{:S(2)}, u32[]{:S(2)}) async-start(bf16[32,2,4096]{2,1,0:T(2,128)(2,1)} %copy.68), calls=%async_computation | async-start | bytes 1048576 | tf_op jit(solution)/shard_map/all_to_all | solution.py:45
  25.2 17.8 %all-to-all-done = bf16[32,2,4096]{2,1,0:T(2,128)(2,1)S(1)} async-done(((bf16[32,2,4096]{2,1,0:T(2,128)(2,1)}), bf16[32,2,4096]{2,1,0:T(2,128)(2,1)S(1)}, u32[]{:S(2)}, u32[]{:S(2)}) %all-to-all-start) | async-done | bytes 524320 | tf_op jit(solution)/shard_map/all_to_all | solution.py:45
  44.2 50.9 %all-gather.4.cloned.1.call-done = bf16[256,4096]{1,0:T(8,128)(2,1)} async-done(((bf16[32,4096]{1,0:T(8,128)(2,1)}), bf16[256,4096]{1,0:T(8,128)(2,1)}) %all-gather.4.cloned.1.call-update) | async-done | bytes 2097168 | tf_op jit(solution)/shard_map/all_gather | solution.py:61
  95.2 3.0 fusion.20
  99.8 25.7 %all-gather.1 = bf16[1536,256]{1,0:T(8,128)(2,1)S(1)} all-gather(bf16[192,256]{1,0:T(8,128)(2,1)S(1)} %get-tuple-element.14), channel_id=3, replica_groups=mesh['dp'=8,'expert'=32] {'dp'}, dimensions={0}, use_global_device_ids=true | all-gather | bytes 884736 | tf_op jit(solution)/shard_map/all_gather | solution.py:67
  129.4 8.5 %all_to_all.84 = bf16[8,2,8192]{2,1,0:T(2,128)(2,1)S(1)} all-to-all(bf16[8,2,8192]{2,1,0:T(2,128)(2,1)S(1)} %reshape.320), channel_id=1, replica_groups=mesh['dp'=8,'expert'=32] {'dp'}, dimensions={0} | all-to-all | bytes 524288 | tf_op jit(solution)/shard_map/all_to_all | solution.py:71
  140.8 5.0 reduce.5
  146.9 17.0 %all-to-all-start.2 = ((bf16[32,2,4096]{2,1,0:T(2,128)(2,1)}), bf16[32,2,4096]{2,1,0:T(2,128)(2,1)}, u32[]{:S(2)}, u32[]{:S(2)}) async-start(bf16[32,2,4096]{2,1,0:T(2,128)(2,1)} %reshape.322), calls=%async_computation.2 | async-start | bytes 1048576 | tf_op jit(solution)/shard_map/all_to_all | solution.py:75
  165.6 16.4 %all-to-all-done.2 = bf16[32,2,4096]{2,1,0:T(2,128)(2,1)} async-done(((bf16[32,2,4096]{2,1,0:T(2,128)(2,1)}), bf16[32,2,4096]{2,1,0:T(2,128)(2,1)}, u32[]{:S(2)}, u32[]{:S(2)}) %all-to-all-start.2) | async-done | bytes 524320 | tf_op jit(solution)/shard_map/all_to_all | solution.py:75
  182.1 3.6 reshape.323
  185.7 4.0 convert_reduce_fusion
  191.5 2.4 multiply_reduce_fusion
  194.5 23.2 %all_to_all.85 = bf16[32,2,4096]{2,1,0:T(2,128)(2,1)} all-to-all(bf16[32,2,4096]{2,1,0:T(2,128)(2,1)S(1)} %copy.75), channel_id=1, replica_groups=mesh['dp'=8,'expert'=32] {'expert'}, dimensions={0} | all-to-all | bytes 1048576 | tf_op jit(solution)/shard_map/all_to_all | solution.py:46
  221.7 5.0 copy.76
  226.8 24.4 %reduce.6 = bf16[4096,32]{1,0:T(8,128)(2,1)} reduce(bf16[4096,1,32]{2,1,0:T(2,128)(2,1)} %bitcast.232, bf16[]{:T(256)} %broadcast.157), dimensions={1}, to_apply=%bitcast.192.reduce_sub_computation | reduce | bytes 524290
  251.2 3.1 reshape.324
  254.3 10.2 %all_to_all.86 = bf16[8,2,8192]{2,1,0:T(2,128)(2,1)} all-to-all(bf16[8,2,8192]{2,1,0:T(2,128)(2,1)} %reshape.324), channel_id=1, replica_groups=mesh['dp'=8,'expert'=32] {'dp'}, dimensions={0} | all-to-all | bytes 524288 | tf_op jit(solution)/shard_map/all_to_all | solution.py:76
  264.5 5.2 reshape.325
  269.6 5.1 copy.77
  278.8 39.2 %reduce-scatter.3.cloned.1.call-done = f32[192,1,256]{2,0,1:T(8,128)} async-done(((f32[1536,1,256]{2,0,1:T(8,128)}), f32[192,1,256]{2,0,1:T(8,128)}) %reduce-scatter.3.cloned.1.call-update) | async-done | bytes 196624 | tf_op jit(solution)/shard_map/reduce_scatter | solution.py:77
  321.4 2.7 fusion
  324.1 95.9 %reduce-scatter.5.cloned.1.call-done = f32[512,1,256]{0,2,1:T(8,128)} async-done(((f32[4096,1,256]{0,2,1:T(8,128)}), f32[512,1,256]{0,2,1:T(8,128)}) %reduce-scatter.5.cloned.1.call-update) | async-done | bytes 524304 | tf_op jit(solution)/shard_map/reduce_scatter | solution.py:97
  422.3 3.8 reduce.7
  428.0 4.0 all-to-all-start.5
  435.0 3.2 all-to-all-done.5
  444.4 5.7 reduce.8
  452.2 11.4 %all-to-all-start.6 = ((bf16[32,2,4096]{2,1,0:T(2,128)(2,1)}), bf16[32,2,4096]{2,1,0:T(2,128)(2,1)}, u32[]{:S(2)}, u32[]{:S(2)}) async-start(bf16[32,2,4096]{2,1,0:T(2,128)(2,1)} %reshape.328), calls=%async_computation.8 | async-start | bytes 1048576 | tf_op jit(solution)/shard_map/all_to_all | solution.py:109
  466.2 3.1 fusion.9
  474.5 7.4 %all-to-all-done.6 = bf16[32,2,4096]{2,1,0:T(2,128)(2,1)} async-done(((bf16[32,2,4096]{2,1,0:T(2,128)(2,1)}), bf16[32,2,4096]{2,1,0:T(2,128)(2,1)}, u32[]{:S(2)}, u32[]{:S(2)}) %all-to-all-start.6) | async-done | bytes 524320 | tf_op jit(solution)/shard_map/all_to_all | solution.py:109
  481.9 3.6 reshape.329
  485.5 3.9 bitcast_reduce_fusion
  493.1 226.2 %all-reduce.2.cloned.1.call-done = f32[4096,32]{0,1:T(8,128)} async-done(((f32[4096,32]{0,1:T(8,128)}), f32[4096,32]{0,1:T(8,128)}) %all-reduce.2.cloned.1.call-update) | async-done | bytes 524304 | tf_op jit(solution)/shard_map/psum | solution.py:122
  (92 shorter events, 60.1 us)
Async XLA Ops:
  7.2 91.0 %copy-start = (bf16[1,192,4096]{2,1,0:T(8,128)(2,1)S(1)}, bf16[1,192,4096]{2,1,0:T(8,128)(2,1)}, u32[]{:S(2)}) copy-start(bf16[1,192,4096]{2,1,0:T(8,128)(2,1)} %param.12) | copy-start | bytes 4718596
  12.6 30.5 %all-to-all-start = ((bf16[32,2,4096]{2,1,0:T(2,128)(2,1)}), bf16[32,2,4096]{2,1,0:T(2,128)(2,1)S(1)}, u32[]{:S(2)}, u32[]{:S(2)}) async-start(bf16[32,2,4096]{2,1,0:T(2,128)(2,1)} %copy.68), calls=%async_computation | async-start | bytes 1048576 | tf_op jit(solution)/shard_map/all_to_all | solution.py:45
  25.2 70.0 %all-gather.4.cloned.1.call-start = ((), (), s32[]{:S(2)}) async-start(), calls=%async_computation.12 | async-start | bytes 2359296 | tf_op jit(solution)/shard_map/all_gather | solution.py:61
  25.2 194.5 %copy-start.13 = (s32[32]{0:T(128)}, s32[32]{0:T(128)S(1)}, u32[]{:S(2)}) copy-start(s32[32]{0:T(128)S(1)} %add_bitcast_fusion) | copy-start | bytes 388
  95.1 3.1 copy-start.1
  98.2 1.6 copy-start.11
  98.2 27.2 %copy-start.3 = (bf16[1,1536,512]{2,1,0:T(8,128)(2,1)S(1)}, bf16[1,1536,512]{2,1,0:T(8,128)(2,1)}, u32[]{:S(2)}) copy-start(bf16[1,1536,512]{2,1,0:T(8,128)(2,1)} %param.13) | copy-start | bytes 4718596
  140.8 23.2 %copy-start.5 = (bf16[1,64,4096]{2,1,0:T(8,128)(2,1)S(1)}, bf16[1,64,4096]{2,1,0:T(8,128)(2,1)}, u32[]{:S(2)}) copy-start(bf16[1,64,4096]{2,1,0:T(8,128)(2,1)} %param.7) | copy-start | bytes 1572868
  146.9 35.1 %all-to-all-start.2 = ((bf16[32,2,4096]{2,1,0:T(2,128)(2,1)}), bf16[32,2,4096]{2,1,0:T(2,128)(2,1)}, u32[]{:S(2)}, u32[]{:S(2)}) async-start(bf16[32,2,4096]{2,1,0:T(2,128)(2,1)} %reshape.322), calls=%async_computation.2 | async-start | bytes 1048576 | tf_op jit(solution)/shard_map/all_to_all | solution.py:75
  163.9 154.1 %reduce-scatter.3.cloned.1.call-start = ((), (), s32[]{:S(2)}) async-start(), calls=%async_computation.9 | async-start | bytes 1769472 | tf_op jit(solution)/shard_map/reduce_scatter | solution.py:77
  165.6 25.9 %copy-start.14 = (f32[32,1,2]{0,2,1:T(2,128)}, f32[32,1,2]{0,2,1:T(2,128)S(1)}, u32[]{:S(2)}) copy-start(f32[32,1,2]{0,2,1:T(2,128)S(1)} %copy.87) | copy-start | bytes 772
  274.8 2.0 copy-start.4
  276.1 0.7 copy-start.6
  278.6 141.5 %reduce-scatter.5.cloned.1.call-start = ((), (), s32[]{:S(2)}) async-start(), calls=%async_computation.10 | async-start | bytes 4718592 | tf_op jit(solution)/shard_map/reduce_scatter | solution.py:97
  319.2 2.2 copy-start.9
  428.0 10.3 %all-to-all-start.5 = ((bf16[8,2,8192]{2,1,0:T(2,128)(2,1)}), bf16[8,2,8192]{2,1,0:T(2,128)(2,1)}, u32[]{:S(2)}, u32[]{:S(2)}) async-start(bf16[8,2,8192]{2,1,0:T(2,128)(2,1)} %reshape.326), calls=%async_computation.7 | async-start | bytes 524288 | tf_op jit(solution)/shard_map/all_to_all | solution.py:105
  452.2 29.6 %all-to-all-start.6 = ((bf16[32,2,4096]{2,1,0:T(2,128)(2,1)}), bf16[32,2,4096]{2,1,0:T(2,128)(2,1)}, u32[]{:S(2)}, u32[]{:S(2)}) async-start(bf16[32,2,4096]{2,1,0:T(2,128)(2,1)} %reshape.328), calls=%async_computation.8 | async-start | bytes 1048576 | tf_op jit(solution)/shard_map/all_to_all | solution.py:109
  463.7 255.6 %all-reduce.2.cloned.1.call-start = ((), (), s32[]{:S(2)}) async-start(), calls=%async_computation.11 | async-start | bytes 1048576 | tf_op jit(solution)/shard_map/psum | solution.py:122
  466.2 3.1 copy-start.7
  469.3 1.7 copy-start.2
  469.3 1.7 copy-start.10
  489.4 2.2 copy-start.8
  489.4 2.2 copy-start.12
Sparse Core Ops, SparseCore 0:
  44.4 50.7 all-gather.3
  278.7 39.2 reduce-scatter.2
  324.3 95.7 reduce-scatter.4
  469.7 249.5 all-reduce.1
where the time goes:
time: 740 us; the launch traced here: 728 us
  waiting for transfers between devices  457 us (62%)
  blocking collectives  67.6 us (9%)
  local copies, waits for them, and re-layouts  57.2 us (8%)
  other arithmetic  49.7 us (7%)
  starting transfers between devices  45.6 us (6%)
  matrix products  36.2 us (5%)
  between operations  14.4 us (2%)
    psum x1, waiting for transfers between devices, local(): router_grad = lax.psum(router_terms, ('dp', 'expert'))  226 us
    reduce_scatter x1, waiting for transfers between devices, local(): lax.psum_scatter(jnp.einsum('flr,lfd->dlr', hidden_diff, gate_weight, pre...  95.9 us
    all_gather x1, waiting for transfers between devices, local(): all_rows = lax.all_gather(expert_rows, 'dp', axis=1, tiled=True)  50.9 us
    unnamed x5, other arithmetic  41.1 us
    reduce_scatter x1, waiting for transfers between devices, local(): lax.psum_scatter(jnp.einsum('lrc,lfc->flr', gated_cols, down_weight, pref...  39.2 us
    unnamed x47, local copies, waits for them, and re-layouts  28.4 us
    all_gather x1, blocking collectives, local(): act_all = lax.all_gather(activated, 'dp', axis=0, tiled=True)  25.7 us
    all_to_all x1, blocking collectives, local(): lax.all_to_all(gated_slots, 'expert', split_axis=0, concat_axis=1, tiled=...  23.2 us
  transfers between devices with their start and end apart: 8, of which 8 were waited for; matrix products, arithmetic and copies ran while one was open for 3% of the time, Pallas kernels for 0%

commit v1 on v0

v1 whole, which is shorter than its diff:
```python
import functools

import jax
import jax.numpy as jnp
from jax import lax
from jax.experimental import pallas as pl
from jax.experimental.pallas import tpu as pltpu
from jax.sharding import PartitionSpec as P

MOST = 2
QUARTERS = 4
F32 = jnp.float32
BF16 = jnp.bfloat16
VMEM = pl.BlockSpec(memory_space=pltpu.VMEM)
SMEM = pl.BlockSpec(memory_space=pltpu.SMEM)


def iota(shape, dim):
    return lax.broadcasted_iota(jnp.int32, shape, dim)


def nn(a, b):
    return lax.dot_general(a, b, (((1,), (0,)), ((), ())), preferred_element_type=F32)


def nt(a, b):
    return lax.dot_general(a, b, (((1,), (1,)), ((), ())), preferred_element_type=F32)


def tn(a, b):
    return lax.dot_general(a, b, (((0,), (0,)), ((), ())), preferred_element_type=F32)


def pieces(x):
    hi = x.astype(BF16)
    rest = x - hi.astype(F32)
    mid = rest.astype(BF16)
    low = (rest - mid.astype(F32)).astype(BF16)
    return hi, mid, low


def call(kernel, outs, args, limit=40, **params):
    return pl.pallas_call(
        kernel,
        out_shape=tuple(jax.ShapeDtypeStruct(s, d) for s, d in outs),
        in_specs=[SMEM if a.ndim == 1 else VMEM for a in args],
        out_specs=tuple(VMEM for _ in outs),
        compiler_params=pltpu.CompilerParams(vmem_limit_bytes=limit * 2**20),
        **params,
    )(*args)


def send_kernel(src_ref, table_ref, tok_ref, grad_ref, router_ref, x_ref, sel_ref, gsel_ref, gates_ref):
    tok_count, width = tok_ref.shape
    experts, cap = table_ref.shape
    part = width // QUARTERS
    slots = experts * MOST * QUARTERS
    gates = jax.nn.sigmoid(nn(tok_ref[...], router_ref[...]))
    gates_ref[...] = gates
    table = table_ref[...]
    owner = table // tok_count
    offset = table - owner * tok_count
    mine = (owner == src_ref[0]).astype(F32)
    before = (iota((cap, cap), 0) < iota((cap, cap), 1)).astype(BF16)
    rank = nn(mine.astype(BF16), before)
    col = iota((experts, slots), 1)
    own_col = (col // (MOST * QUARTERS)) == iota((experts, slots), 0)
    col_rank = (col // QUARTERS) % MOST
    wanted = jnp.zeros((1, slots), F32)
    for m in range(MOST):
        chosen = jnp.sum(
            jnp.where(rank == m, mine, 0.0) * (offset + 1).astype(F32), axis=1, keepdims=True
        )
        wanted += jnp.sum(
            jnp.where(own_col & (col_rank == m), chosen, 0.0), axis=0, keepdims=True
        )
    sel = (iota((tok_count, slots), 0) + 1).astype(F32) == wanted
    expand = own_col.astype(BF16)
    gate_exp = sum(nn(p, expand) for p in pieces(gates))
    gsel = jnp.where(sel, gate_exp, 0.0)
    sel_low = sel.astype(BF16)
    sel_ref[...] = sel_low
    gsel_ref[...] = gsel
    ones = jnp.ones((tok_count, 128), BF16)
    slot_gate = sum(tn(p, ones) for p in pieces(gsel))
    quarter = iota((tok_count, slots), 1) % QUARTERS
    pick = jnp.concatenate(
        [jnp.where(quarter == q, sel_low, jnp.zeros_like(sel_low)) for q in range(QUARTERS)], axis=0
    )
    for half, ref in enumerate((tok_ref, grad_ref)):
        rows = jnp.concatenate([ref[:, q * part : (q + 1) * part] for q in range(QUARTERS)], axis=0)
        got = tn(pick, rows)
        if half == 1:
            got = got * slot_gate[:, :1]
        x_ref[:, half * part : (half + 1) * part] = got.astype(BF16)


def own_rows(src_ref, table_ref, tok_count):
    experts, cap = table_ref.shape
    owner = table_ref[...] // tok_count
    row = jnp.sum(
        jnp.where(iota((experts, cap), 0) == src_ref[0], owner, 0).astype(F32), axis=0, keepdims=True
    )
    a, b = iota((cap, cap), 0), iota((cap, cap), 1)
    col = jnp.sum(jnp.where(a == b, row, 0.0), axis=1, keepdims=True)
    same = row == col
    rank_col = jnp.sum(jnp.where(same & (b < a), 1.0, 0.0), axis=1, keepdims=True)
    rank_row = jnp.sum(jnp.where(same & (a < b), 1.0, 0.0), axis=0, keepdims=True)
    step = MOST * QUARTERS
    return (
        (row * step + rank_row * QUARTERS).astype(jnp.int32),
        (col * step + rank_col * QUARTERS).astype(jnp.int32),
    )


def pack_kernel(tok_count, src_ref, table_ref, x_ref, a_ref):
    cap = table_ref.shape[1]
    slots, twice = x_ref.shape
    part = twice // 2
    n_dp = a_ref.shape[0]
    _, col = own_rows(src_ref, table_ref, tok_count)
    ids = jnp.concatenate([col + q for q in range(QUARTERS)], axis=0)
    pick = (iota((QUARTERS * cap, slots), 1) == ids).astype(BF16)
    y = nn(pick, x_ref[...]).astype(BF16)
    width = part * QUARTERS
    cols = width // n_dp
    for d in range(n_dp):
        for q in range(QUARTERS):
            a_ref[d, :, q * part : (q + 1) * part] = y[q * cap : (q + 1) * cap, :part]
        q, start = divmod(d * cols, part)
        a_ref[d, :, width : width + cols] = y[q * cap : (q + 1) * cap, part + start : part + start + cols]


def hidden_kernel(src_ref, a_ref, gate_ref, up_ref, down_ref, router_ref, b_ref, h_ref, u_ref, rest_ref):
    units, width = gate_ref.shape
    rows_n = a_ref.shape[0]
    n_dp = b_ref.shape[0]
    rows = a_ref[:, :width]
    h = nt(gate_ref[...], rows)
    u = nt(up_ref[...], rows)
    h_ref[...] = h
    u_ref[...] = u
    act = (h * jax.nn.sigmoid(h) * u).astype(BF16)
    gated = a_ref[:, width:]
    logits = nn(rows, router_ref[...])
    own = jnp.where(iota(logits.shape, 1) == src_ref[0], logits, 0.0)
    gate = jax.nn.sigmoid(jnp.sum(own, axis=1, keepdims=True))
    rest_ref[...] = jnp.broadcast_to(1.0 - gate, rest_ref.shape)
    for d in range(n_dp):
        b_ref[d, :, :rows_n] = act
        b_ref[d, :, rows_n:] = nt(down_ref[d * units : (d + 1) * units, :], gated).astype(BF16)


def diff_kernel(b_ref, h_ref, u_ref, a_ref, gate_ref, up_ref, down_ref, rest_ref, c_ref, dh_ref, du_ref):
    n_dp, units, twice = b_ref.shape
    rows_n = twice // 2
    width = gate_ref.shape[1]
    cap = rows_n // n_dp
    cols = down_ref.shape[1]
    dact = b_ref[0, :, rows_n:].astype(F32)
    for d in range(1, n_dp):
        dact = dact + b_ref[d, :, rows_n:].astype(F32)
    h, u = h_ref[...], u_ref[...]
    sig = jax.nn.sigmoid(h)
    dh = (dact * u * sig * (1.0 + h * (1.0 - sig))).astype(BF16)
    du = (dact * h * sig).astype(BF16)
    dh_ref[...] = dh
    du_ref[...] = du
    out = tn(b_ref[0, :, :rows_n], down_ref[:units, :])
    for d in range(1, n_dp):
        out = out + tn(b_ref[d, :, :rows_n], down_ref[d * units : (d + 1) * units, :])
    out = out.astype(BF16)
    c_ref[:, width : width + cols] = out
    dgate = jnp.sum(a_ref[:, width:].astype(F32) * out.astype(F32), axis=1, keepdims=True)
    dlogit = dgate * rest_ref[:, :1]
    lane = iota((cap, 128), 1)
    packed = jnp.zeros((cap, 128), F32)
    for p, piece in enumerate(pieces(dlogit)):
        piece = piece.astype(F32)
        for g in range(n_dp):
            packed = jnp.where(lane == p * n_dp + g, piece[g * cap : (g + 1) * cap], packed)
    c_ref[:, width + cols :] = jnp.concatenate([packed] * n_dp, axis=0).astype(BF16)
    dht, dut = dh.T, du.T
    step = 512
    for j in range(0, width, step):
        c_ref[:, j : j + step] = (
            nn(dht, gate_ref[:, j : j + step]) + nn(dut, up_ref[:, j : j + step])
        ).astype(BF16)


def weight_kernel(dh_ref, du_ref, b_ref, a_ref, gg_ref, ug_ref, dg_ref):
    units, width = gg_ref.shape
    n_dp = b_ref.shape[0]
    rows_n = a_ref.shape[0]
    step = 512
    dh, du = dh_ref[...], du_ref[...]
    for j in range(0, width, step):
        gg_ref[:, j : j + step] = nn(dh, a_ref[:, j : j + step]).astype(BF16)
        ug_ref[:, j : j + step] = nn(du, a_ref[:, j : j + step]).astype(BF16)
    gated = a_ref[:, width:]
    for d in range(n_dp):
        dg_ref[d * units : (d + 1) * units, :] = nn(b_ref[d, :, :rows_n], gated).astype(BF16)


def back_kernel(tok_count, src_ref, table_ref, c_ref, a_ref, z_ref):
    n_dp, cap, _ = c_ref.shape
    slots = z_ref.shape[0]
    part = 1024
    width = part * QUARTERS
    cols = width // n_dp
    row, _ = own_rows(src_ref, table_ref, tok_count)
    ids = jnp.concatenate([row + q for q in range(QUARTERS)], axis=1)
    place = (iota((slots, QUARTERS * cap), 0) == ids).astype(BF16)
    per = part // cols
    outs = jnp.concatenate(
        [
            jnp.concatenate([c_ref[q * per + i, :, width : width + cols] for i in range(per)], axis=1)
            for q in range(QUARTERS)
        ],
        axis=0,
    )
    z_ref[:, :part] = nn(place, outs).astype(BF16)
    diffs = []
    for q in range(QUARTERS):
        total = c_ref[0, :, q * part : (q + 1) * part].astype(F32)
        for d in range(1, n_dp):
            total = total + c_ref[d, :, q * part : (q + 1) * part].astype(F32)
        diffs.append(total.astype(BF16))
    z_ref[:, part : 2 * part] = nn(place, jnp.concatenate(diffs, axis=0)).astype(BF16)
    packed = c_ref[0, :, width + cols :].astype(F32)
    for d in range(1, n_dp):
        packed = packed + c_ref[d, :, width + cols :].astype(F32)
    rows_n = n_dp * cap
    lane = iota((128, rows_n), 0)
    spread = ((lane % n_dp == iota((128, rows_n), 1) // cap) & (lane < 3 * n_dp)).astype(BF16)
    dlogit = sum(nn(p, spread) for p in pieces(packed))
    dlogit = jnp.sum(
        jnp.where(iota((cap, rows_n), 0) == iota((cap, rows_n), 1) % cap, dlogit, 0.0),
        axis=0,
        keepdims=True,
    )
    terms = jnp.concatenate(
        [p.astype(F32) for p in pieces(dlogit)] + [jnp.zeros((5, rows_n), F32)], axis=0
    ).astype(BF16)
    chunk = width // 8
    column = jnp.concatenate(
        [
            jnp.sum(nn(terms, a_ref[:, i * chunk : (i + 1) * chunk]), axis=0, keepdims=True)
            for i in range(8)
        ],
        axis=0,
    )
    z_ref[:, 2 * part :] = jnp.concatenate([column] * (slots // 8), axis=0).astype(BF16)


def take_kernel(d_ref, sel_ref, gsel_ref, gates_ref, grad_ref, router_ref, mixed_ref, tgrad_ref):
    tok_count, width = grad_ref.shape
    slots = d_ref.shape[0]
    experts = gates_ref.shape[1]
    part = width // QUARTERS
    sel, gsel = sel_ref[...], gsel_ref[...]
    quarter = iota((tok_count, slots), 1) % QUARTERS
    outs = d_ref[:, :part]
    weights = pieces(gsel)
    zero = jnp.zeros_like(sel)
    hits = jnp.zeros((tok_count, slots), F32)
    for q in range(QUARTERS):
        here = quarter == q
        hits += jnp.where(here, nt(grad_ref[:, q * part : (q + 1) * part], outs), 0.0)
        mixed_ref[:, q * part : (q + 1) * part] = sum(
            nn(jnp.where(here, w, zero), outs) for w in weights
        ).astype(BF16)
    hits = jnp.where(sel != 0, hits, 0.0)
    collect = (iota((slots, experts), 0) // (MOST * QUARTERS) == iota((slots, experts), 1)).astype(BF16)
    gates = gates_ref[...]
    dlogit = sum(nn(p, collect) for p in pieces(hits)) * gates * (1.0 - gates)
    terms = pieces(dlogit)
    for q in range(QUARTERS):
        span = slice(q * part, (q + 1) * part)
        total = nn(jnp.where(quarter == q, sel, zero), d_ref[:, part : 2 * part])
        for w in terms:
            total = total + nt(w, router_ref[span, :])
        tgrad_ref[:, span] = total.astype(BF16)


def local(tokens, out_grad, router, choice_index, gate_weight, up_weight, down_weight):
    tok, grad, table = tokens[0], out_grad[0], choice_index[0]
    gate, up, down = gate_weight[0], up_weight[0], down_weight[0]
    tok_count, width = tok.shape
    experts, cap = table.shape
    units, cols = gate.shape[0], down.shape[1]
    n_dp = lax.axis_size("dp")
    rows_n = n_dp * cap
    slots = experts * MOST * QUARTERS
    src = lax.axis_index("expert").astype(jnp.int32).reshape(1)

    def swap(x, axis):
        return lax.all_to_all(x, axis, split_axis=0, concat_axis=0, tiled=True)

    x, sel, gsel, gates = call(
        send_kernel,
        [
            ((slots, width // 2), BF16),
            ((tok_count, slots), BF16),
            ((tok_count, slots), F32),
            ((tok_count, experts), F32),
        ],
        (src, table, tok, grad, router),
    )
    x = swap(x.reshape(experts, MOST * QUARTERS, width // 2), "expert").reshape(x.shape)
    (a,) = call(
        functools.partial(pack_kernel, tok_count),
        [((n_dp, cap, width + cols), BF16)],
        (src, table, x),
    )
    a = swap(a, "dp").reshape(rows_n, width + cols)
    b, h, u, rest = call(
        hidden_kernel,
        [
            ((n_dp, units, 2 * rows_n), BF16),
            ((units, rows_n), F32),
            ((units, rows_n), F32),
            ((rows_n, 128), F32),
        ],
        (src, a, gate, up, down, router),
    )
    b = swap(b, "dp")
    c, dh, du = call(
        diff_kernel,
        [
            ((rows_n, width + cols + 128), BF16),
            ((units, rows_n), BF16),
            ((units, rows_n), BF16),
        ],
        (b, h, u, a, gate, up, down, rest),
    )
    c = swap(c.reshape(n_dp, cap, width + cols + 128), "dp")
    gate_grad, up_grad, down_grad = call(
        weight_kernel,
        [((units, width), BF16), ((units, width), BF16), ((n_dp * units, cols), BF16)],
        (dh, du, b, a),
    )
    (z,) = call(
        functools.partial(back_kernel, tok_count),
        [((slots, width // 2 + width // 8), BF16)],
        (src, table, c, a),
    )
    z = swap(z.reshape(experts, MOST * QUARTERS, -1), "expert")
    router_grad = z[:, :, width // 2 :].reshape(experts, width).T.astype(F32)
    mixed, token_grad = call(
        take_kernel,
        [((tok_count, width), BF16), ((tok_count, width), BF16)],
        (z.reshape(slots, -1), sel, gsel, gates, grad, router),
    )
    return (
        mixed[None],
        token_grad[None],
        router_grad,
        gate_grad[None],
        up_grad[None],
        down_grad[None],
    )


def solution(mesh):
    in_specs = (
        P("dp", "expert", None),
        P("dp", "expert", None),
        P(),
        P("dp", None, None),
        P("expert", "dp", None),
        P("expert", "dp", None),
        P("expert", None, "dp"),
    )
    out_specs = (
        P("dp", "expert", None),
        P("dp", "expert", None),
        P(),
        P("expert", "dp", None),
        P("expert", "dp", None),
        P("expert", None, "dp"),
    )
    return jax.shard_map(local, mesh=mesh, in_specs=in_specs, out_specs=out_specs, check_vma=False)
```

time: 740 us -> 193 us (0.26); the launches traced: 728 us -> 192 us
  waiting for transfers between devices: 457 us -> 28.4 us
  blocking collectives: 67.6 us -> 127 us
  local copies, waits for them, and re-layouts: 57.2 us -> 6.73 us
  other arithmetic: 49.7 us -> 1 us
  matrix products: 36.2 us -> 0 us
  starting transfers between devices: 45.6 us -> 11.8 us
  Pallas kernels: 0 us -> 16.5 us
  between operations: 14.4 us -> 0.83 us
    psum x1 -> x0, waiting for transfers between devices: 226 us -> none  [local(): router_grad = lax.psum(router_terms, ('dp', 'expert'))]
    reduce_scatter x2 -> x0, waiting for transfers between devices: 135 us -> none  [the longest x1 95.9 us: local(): lax.psum_scatter(jnp.einsum('flr,lfd->dlr', hidden_diff, gate_weight, pre...]
    all_to_all x3 -> x4, blocking collectives: 41.9 us -> 127 us  [swap(): return lax.all_to_all(x, axis, split_axis=0, concat_axis=0, tiled=True)]
    all_gather x1 -> x0, waiting for transfers between devices: 50.9 us -> none  [local(): all_rows = lax.all_gather(expert_rows, 'dp', axis=1, tiled=True)]
    unnamed x5 -> x0, other arithmetic: 41.1 us -> none
    dot_general x23 -> x0, matrix products: 36.2 us -> none  [the longest x1 3.06 us: local(): jnp.einsum('emt,emd->td', select, weighted, precision=highest)]
    all_to_all x4 -> x1, starting transfers between devices: 45.1 us -> 11.8 us  [swap(): return lax.all_to_all(x, axis, split_axis=0, concat_axis=0, tiled=True)]
    all_gather x1 -> x0, blocking collectives: 25.7 us -> none  [local(): act_all = lax.all_gather(activated, 'dp', axis=0, tiled=True)]
  transfers between devices with their start and end apart: 8 -> 1, of which waited for: 8 -> 1; matrix products, arithmetic and copies ran while one was open for 3% -> 0% of each run, Pallas kernels for 0% -> 2%
where the time goes in v1:
time: 193 us; the launch traced here: 192 us
  blocking collectives  127 us (66%)
  waiting for transfers between devices  28.4 us (15%)
  Pallas kernels  16.5 us (9%)
  starting transfers between devices  11.8 us (6%)
  local copies, waits for them, and re-layouts  6.73 us (3%)
    all_to_all x4, blocking collectives, swap(): return lax.all_to_all(x, axis, split_axis=0, concat_axis=0, tiled=True)  127 us
    all_to_all x1, waiting for transfers between devices, swap(): return lax.all_to_all(x, axis, split_axis=0, concat_axis=0, tiled=True)  28.4 us
    pallas_call x7, Pallas kernels, call(): pl.pallas_call(kernel, out_shape=tuple((jax.ShapeDtypeStruct(s, d) for s,...  16.5 us
    all_to_all x1, starting transfers between devices, swap(): return lax.all_to_all(x, axis, split_axis=0, concat_axis=0, tiled=True)  11.8 us
    unnamed x36, local copies, waits for them, and re-layouts  6.73 us
  transfers between devices with their start and end apart: 1, of which 1 were waited for; matrix products, arithmetic and copies ran while one was open for 0% of the time, Pallas kernels for 2%

profile of v1, /device:TPU:1, one launch (start us, length us, event | category | flops | bytes accessed | tf_op | source)
XLA Modules:
  0.0 192.1 jit_solution(18074994350533132389)
XLA Ops:
  0.6 0.0 copy-start.6
  0.6 0.0 copy-start.8
  0.7 1.5 copy.13.router_ref
  2.2 0.0 copy-done.6
  2.2 0.0 copy-start.9
  2.2 0.7 copy-done.9
  2.9 1.0 shard_map.118
  3.9 0.0 copy-start.13
  3.9 0.0 copy-start.15
  4.0 41.3 %all_to_all.25 = bf16[32,8,2048]{2,1,0:T(8,128)(2,1)S(1)} all-to-all(bf16[32,8,2048]{2,1,0:T(8,128)(2,1)S(1)} %bitcast.37), channel_id=1, replica_groups=mesh['dp'=8,'expert'=32] {'expert'}, dimensions={0} | all-to-all | bytes 2097152 | tf_op jit(solution)/shard_map/all_to_all | solution.py:298
  45.2 0.6 shard_map.119
  45.8 0.0 copy-start.2
  45.8 0.0 copy-start.3
  45.8 0.0 copy-start.4
  45.8 33.7 %all_to_all.26 = bf16[8,32,4608]{2,1,0:T(8,128)(2,1)S(1)} all-to-all(bf16[8,32,4608]{2,1,0:T(8,128)(2,1)S(1)} %shard_map.119), channel_id=1, replica_groups=mesh['dp'=8,'expert'=32] {'dp'}, dimensions={0} | all-to-all | bytes 4718592 | tf_op jit(solution)/shard_map/all_to_all | solution.py:298
  79.5 2.7 %shard_map.120 = (bf16[8,192,512]{2,1,0:T(8,128)(2,1)S(1)}, f32[192,256]{1,0:T(8,128)S(1)}, f32[192,256]{1,0:T(8,128)S(1)}, f32[256,128]{1,0:T(8,128)S(1)}) custom-call(s32[1]{0:T(128)} %bitcast.src_ref, bf16[256,4608]{1,0:T(8,128)(2,1)S(1)} %bitcast.22, bf16[192,4096]{1,0:T(8,128)(2,1)S(1)} %bitcast.26, bf16[192,4096]{1,0:T(8,128)(2,1)S(1)} %bitcast.28, ...), custom_call_target="tpu_custom_call" | custom-call | tf_op jit(solution)/shard_map/pallas_call | solution.py:43
  82.3 21.6 %all_to_all.27.b_ref = bf16[8,192,512]{2,1,0:T(8,128)(2,1)S(1)} all-to-all(bf16[8,192,512]{2,1,0:T(8,128)(2,1)S(1)} %get-tuple-element.23), channel_id=1, replica_groups=mesh['dp'=8,'expert'=32] {'dp'}, dimensions={0} | all-to-all | bytes 3145728 | tf_op jit(solution)/shard_map/all_to_all | solution.py:298
  103.9 1.9 %shard_map.121 = (bf16[256,4736]{1,0:T(8,128)(2,1)S(1)}, bf16[192,256]{1,0:T(8,128)(2,1)S(1)}, bf16[192,256]{1,0:T(8,128)(2,1)S(1)}) custom-call(bf16[8,192,512]{2,1,0:T(8,128)(2,1)S(1)} %all_to_all.27.b_ref, f32[192,256]{1,0:T(8,128)S(1)} %get-tuple-element.24.h_ref, f32[192,256]{1,0:T(8,128)S(1)} %get-tuple-element.25.u_ref, ...), custom_call_target="tpu_custom_call" | custom-call | tf_op jit(solution)/shard_map/pallas_call | solution.py:43
  105.8 0.0 copy-start.11
  105.9 0.0 copy-start.10
  105.9 30.3 %all_to_all.28.c_ref = bf16[8,32,4736]{2,1,0:T(8,128)(2,1)S(1)} all-to-all(bf16[8,32,4736]{2,1,0:T(8,128)(2,1)S(1)} %bitcast.34), channel_id=1, replica_groups=mesh['dp'=8,'expert'=32] {'dp'}, dimensions={0} | all-to-all | bytes 4849664 | tf_op jit(solution)/shard_map/all_to_all | solution.py:298
  136.2 1.1 shard_map.122
  137.3 1.0 copy-done.5
  138.3 11.8 %all-to-all-start.4 = ((bf16[32,8,2560]{2,1,0:T(8,128)(2,1)}), bf16[32,8,2560]{2,1,0:T(8,128)(2,1)}, u32[]{:S(2)}, u32[]{:S(2)}) async-start(bf16[32,8,2560]{2,1,0:T(8,128)(2,1)} %bitcast.32), calls=%async_computation.4 | async-start | bytes 2621440 | tf_op jit(solution)/shard_map/all_to_all | solution.py:298
  150.1 0.0 copy-start.1
  150.1 1.4 copy-done.1
  151.5 0.9 copy-done.12
  152.4 3.3 %shard_map.124 = (bf16[192,4096]{1,0:T(8,128)(2,1)}, bf16[192,4096]{1,0:T(8,128)(2,1)}, bf16[1536,512]{1,0:T(8,128)(2,1)}) custom-call(bf16[192,256]{1,0:T(8,128)(2,1)S(1)} %get-tuple-element.33.dh_ref, bf16[192,256]{1,0:T(8,128)(2,1)S(1)} %copy-done.12, bf16[8,192,512]{2,1,0:T(8,128)(2,1)S(1)} %copy-done.1, bf16[256,4608]{1,0:T(8,128)(2,1)S(1)} %bitcast.25), custom_call_target="tpu_custom_call" | custom-call | tf_op jit(solution)/shard_map/pallas_call | solution.py:43
  155.8 28.4 %all-to-all-done.4 = bf16[32,8,2560]{2,1,0:T(8,128)(2,1)} async-done(((bf16[32,8,2560]{2,1,0:T(8,128)(2,1)}), bf16[32,8,2560]{2,1,0:T(8,128)(2,1)}, u32[]{:S(2)}, u32[]{:S(2)}) %all-to-all-start.4) | async-done | bytes 1310752 | tf_op jit(solution)/shard_map/all_to_all | solution.py:298
  184.2 1.0 slice_convert_fusion
  185.2 1.1 copy.16
  186.3 5.8 %shard_map.123 = (bf16[64,4096]{1,0:T(8,128)(2,1)}, bf16[64,4096]{1,0:T(8,128)(2,1)}) custom-call(bf16[256,2560]{1,0:T(8,128)(2,1)} %bitcast.12.d_ref, bf16[64,256]{1,0:T(8,128)(2,1)S(1)} %get-tuple-element.28.sel_ref, f32[64,256]{1,0:T(8,128)S(1)} %copy-done.14, f32[64,32]{1,0:T(8,128)S(1)} %copy-done.16, bf16[64,4096]{1,0:T(8,128)(2,1)S(1)} %bitcast.36, ...), custom_call_target="tpu_custom_call" | custom-call | tf_op jit(solution)/shard_map/pallas_call | solution.py:43
  (18 shorter events, 0.0 us)
Async XLA Ops:
  0.6 1.5 copy-start.6
  0.6 1.5 copy-start.8
  2.2 0.7 copy-start.9
  3.9 41.3 %copy-start.13 = (f32[64,256]{1,0:T(8,128)}, f32[64,256]{1,0:T(8,128)S(1)}, u32[]{:S(2)}) copy-start(f32[64,256]{1,0:T(8,128)S(1)} %get-tuple-element.29.gsel_ref) | copy-start | bytes 196612
  3.9 41.3 %copy-start.15 = (f32[64,32]{1,0:T(8,128)}, f32[64,32]{1,0:T(8,128)S(1)}, u32[]{:S(2)}) copy-start(f32[64,32]{1,0:T(8,128)S(1)} %get-tuple-element.30.gates_ref) | copy-start | bytes 24580
  45.8 33.7 %copy-start.2 = (bf16[1,192,4096]{2,1,0:T(8,128)(2,1)S(1)}, bf16[1,192,4096]{2,1,0:T(8,128)(2,1)}, u32[]{:S(2)}) copy-start(bf16[1,192,4096]{2,1,0:T(8,128)(2,1)} %param.11) | copy-start | bytes 4718596
  45.8 33.7 %copy-start.3 = (bf16[1,192,4096]{2,1,0:T(8,128)(2,1)S(1)}, bf16[1,192,4096]{2,1,0:T(8,128)(2,1)}, u32[]{:S(2)}) copy-start(bf16[1,192,4096]{2,1,0:T(8,128)(2,1)} %param.12) | copy-start | bytes 4718596
  45.8 33.7 %copy-start.4 = (bf16[1,1536,512]{2,1,0:T(8,128)(2,1)S(1)}, bf16[1,1536,512]{2,1,0:T(8,128)(2,1)}, u32[]{:S(2)}) copy-start(bf16[1,1536,512]{2,1,0:T(8,128)(2,1)} %param.13) | copy-start | bytes 4718596
  103.9 1.9 %copy-start = (bf16[8,192,512]{2,1,0:T(8,128)(2,1)}, bf16[8,192,512]{2,1,0:T(8,128)(2,1)S(1)}, u32[]{:S(2)}) copy-start(bf16[8,192,512]{2,1,0:T(8,128)(2,1)S(1)} %all_to_all.27.b_ref) | copy-start | bytes 4718596
  105.8 30.3 %copy-start.11 = (bf16[192,256]{1,0:T(8,128)(2,1)}, bf16[192,256]{1,0:T(8,128)(2,1)S(1)}, u32[]{:S(2)}) copy-start(bf16[192,256]{1,0:T(8,128)(2,1)S(1)} %get-tuple-element.34.du_ref) | copy-start | bytes 294916
  105.9 30.3 %copy-start.10 = (s32[1,32,32]{2,1,0:T(8,128)S(1)}, s32[1,32,32]{2,1,0:T(8,128)}, u32[]{:S(2)}) copy-start(s32[1,32,32]{2,1,0:T(8,128)} %param.10) | copy-start | bytes 12292
  137.3 1.1 copy-start.5
  138.3 45.8 %all-to-all-start.4 = ((bf16[32,8,2560]{2,1,0:T(8,128)(2,1)}), bf16[32,8,2560]{2,1,0:T(8,128)(2,1)}, u32[]{:S(2)}, u32[]{:S(2)}) async-start(bf16[32,8,2560]{2,1,0:T(8,128)(2,1)} %bitcast.32), calls=%async_computation.4 | async-start | bytes 2621440 | tf_op jit(solution)/shard_map/all_to_all | solution.py:298
  150.1 1.4 copy-start.1
  151.5 0.9 copy-start.12
  155.8 30.5 %copy-start.7 = (bf16[1,64,4096]{2,1,0:T(8,128)(2,1)S(1)}, bf16[1,64,4096]{2,1,0:T(8,128)(2,1)}, u32[]{:S(2)}) copy-start(bf16[1,64,4096]{2,1,0:T(8,128)(2,1)} %param.8) | copy-start | bytes 1572868
  155.8 30.5 %copy-start.14 = (f32[64,256]{1,0:T(8,128)S(1)}, f32[64,256]{1,0:T(8,128)}, u32[]{:S(2)}) copy-start(f32[64,256]{1,0:T(8,128)} %copy-done.13) | copy-start | bytes 196612
  155.8 30.5 %copy-start.16 = (f32[64,32]{1,0:T(8,128)S(1)}, f32[64,32]{1,0:T(8,128)}, u32[]{:S(2)}) copy-start(f32[64,32]{1,0:T(8,128)} %copy-done.15) | copy-start | bytes 24580

commit v2 on v0

v2 whole, which is shorter than its diff:
```python
import jax
import jax.numpy as jnp
from jax import lax
from jax.experimental import pallas as pl
from jax.experimental.pallas import tpu as pltpu
from jax.sharding import PartitionSpec as P

MOST = 2
LANES = 128
EMPTY = 1024.0
F32 = jnp.float32
BF16 = jnp.bfloat16
VMEM = pl.BlockSpec(memory_space=pltpu.VMEM)
SMEM = pl.BlockSpec(memory_space=pltpu.SMEM)
FAR = pl.BlockSpec(memory_space=pltpu.HBM)


def iota(shape, dim):
    return lax.broadcasted_iota(jnp.int32, shape, dim)


def nn(a, b):
    return lax.dot_general(a, b, (((1,), (0,)), ((), ())), preferred_element_type=F32)


def nt(a, b):
    return lax.dot_general(a, b, (((1,), (1,)), ((), ())), preferred_element_type=F32)


def tn(a, b):
    return lax.dot_general(a, b, (((0,), (0,)), ((), ())), preferred_element_type=F32)


def pieces(x):
    hi = x.astype(BF16)
    rest = x - hi.astype(F32)
    mid = rest.astype(BF16)
    low = (rest - mid.astype(F32)).astype(BF16)
    return hi, mid, low


def call(kernel, outs, args, far_in=(), far_out=(), scratch=()):
    args = [
        pltpu.with_memory_space_constraint(a, pltpu.HBM) if i in far_in else a for i, a in enumerate(args)
    ]
    return pl.pallas_call(
        kernel,
        out_shape=tuple(
            pltpu.HBM(s, d) if i in far_out else jax.ShapeDtypeStruct(s, d)
            for i, (s, d) in enumerate(outs)
        ),
        in_specs=[SMEM if a.ndim == 1 else FAR if i in far_in else VMEM for i, a in enumerate(args)],
        out_specs=tuple(FAR if i in far_out else VMEM for i in range(len(outs))),
        scratch_shapes=scratch,
        compiler_params=pltpu.CompilerParams(vmem_limit_bytes=40 * 2**20),
    )(*args)


def send_kernel(src_ref, *refs):
    far, x_ref, outs_far, near, near_out, sem = refs[:4], refs[4], refs[5:8], refs[8:12], refs[12:15], refs[15]
    sel_ref, gsel_ref, gates_ref = near_out
    back = [
        pltpu.make_async_copy(a, b, sem.at[len(far) + i])
        for i, (a, b) in enumerate(zip(near_out, outs_far))
    ]
    copies = [pltpu.make_async_copy(a, b, sem.at[i]) for i, (a, b) in enumerate(zip(far, near))]
    for copy in copies:
        copy.start()
    table_ref, tok_ref, grad_ref, router_ref = near
    tok_count, width = tok_ref.shape
    experts, cap = table_ref.shape
    n_dp, slots, _ = x_ref.shape
    chunks = slots // (experts * MOST)
    cols = width // n_dp
    copies[0].wait()
    table = table_ref[...]
    owner = table // tok_count
    offset = table - owner * tok_count
    mine = (owner == src_ref[0]).astype(F32)
    before = (iota((cap, cap), 0) < iota((cap, cap), 1)).astype(BF16)
    rank = nn(mine.astype(BF16), before)
    col = iota((experts, slots), 1)
    own_col = (col // (MOST * chunks)) == iota((experts, slots), 0)
    col_rank = (col // chunks) % MOST
    wanted = jnp.zeros((1, slots), F32)
    for m in range(MOST):
        chosen = jnp.sum(
            jnp.where(rank == m, mine, 0.0) * (offset + 1).astype(F32), axis=1, keepdims=True
        )
        wanted += jnp.sum(
            jnp.where(own_col & (col_rank == m), chosen, 0.0), axis=0, keepdims=True
        )
    sel = (iota((tok_count, slots), 0) + 1).astype(F32) == wanted
    copies[3].wait()
    copies[1].wait()
    gates = jax.nn.sigmoid(nt(tok_ref[...], router_ref[...]))
    gates_ref[...] = gates
    expand = own_col.astype(BF16)
    gate_exp = sum(nn(p, expand) for p in pieces(gates))
    gsel = jnp.where(sel, gate_exp, 0.0)
    sel_low = sel.astype(BF16)
    sel_ref[...] = sel_low
    gsel_ref[...] = gsel
    for copy in back:
        copy.start()
    ones = jnp.ones((tok_count, LANES), BF16)
    slot_gate = sum(tn(p, ones) for p in pieces(gsel))
    slot_empty = (1.0 - tn(sel_low, ones)) * EMPTY
    chunk = iota((tok_count, slots), 1) % chunks
    pick = jnp.concatenate(
        [jnp.where(chunk == c, sel_low, jnp.zeros_like(sel_low)) for c in range(chunks)], axis=0
    )
    copies[2].wait()
    for d in range(n_dp):
        parts = []
        for c in range(chunks):
            span = slice(d * cols + c * LANES, d * cols + (c + 1) * LANES)
            parts.append(jnp.concatenate([tok_ref[:, span], grad_ref[:, span]], axis=1))
        got = tn(pick, jnp.concatenate(parts, axis=0))
        x_ref[d, :, :LANES] = (got[:, :LANES] + slot_empty).astype(BF16)
        x_ref[d, :, LANES:] = (got[:, LANES:] * slot_gate).astype(BF16)
    for copy in back:
        copy.wait()


def pack_kernel(x_ref, down_ref, p_ref, gated_ref, pick_ref):
    n_dp, rows_all, cols = p_ref.shape
    rows_n = gated_ref.shape[0]
    half = rows_all - rows_n
    cap = rows_n // n_dp
    chunks = cols // LANES
    slots = x_ref.shape[0] // n_dp
    lane = iota((slots, LANES), 1)
    row = iota((slots, LANES), 0)
    held = [x_ref[g * slots : (g + 1) * slots, :LANES] < EMPTY / 2 for g in range(n_dp)]
    a, b = iota((slots, slots), 0), iota((slots, slots), 1)
    before = ((b // chunks < a // chunks) & (b % chunks == 0)).astype(BF16)
    place = nn(before, jnp.concatenate([h.astype(BF16) for h in held], axis=1))
    mine = lane // cap == row % chunks
    want = (lane % cap).astype(F32)
    for g in range(n_dp):
        at = jnp.where(mine, place[:, g * LANES : (g + 1) * LANES], -1.0)
        pick = jnp.where(at == want, held[g].astype(F32), 0.0).astype(BF16)
        pick_ref[g * slots : (g + 1) * slots, :] = pick
        y = tn(pick, x_ref[g * slots : (g + 1) * slots, :]).astype(BF16)
        own = slice(g * cap, (g + 1) * cap)
        for c in range(chunks):
            span = slice(c * LANES, (c + 1) * LANES)
            gated_ref[own, span] = y[c * cap : (c + 1) * cap, LANES:]
            for d in range(n_dp):
                p_ref[d, own, span] = y[c * cap : (c + 1) * cap, :LANES]
    gated = gated_ref[...]
    for d in range(n_dp):
        term = nt(down_ref[2 * d * half : 2 * (d + 1) * half, :], gated).astype(BF16)
        p_ref[d, rows_n:, :rows_n] = term[:half]
        p_ref[d, rows_n:, rows_n:] = term[half:]


def hidden_kernel(src_ref, a_ref, gate_ref, up_ref, router_ref, c_ref, dh_ref, du_ref):
    units, width = gate_ref.shape
    experts = router_ref.shape[0]
    n_dp, rows_all, cols = a_ref.shape
    half = units // 2
    rows_n = rows_all - half
    total = jnp.zeros((2 * units + experts, rows_n), F32)
    dact = jnp.zeros((units, rows_n), F32)
    group = 2
    for d in range(0, n_dp, group):
        span = slice(d * cols, (d + group) * cols)
        left = jnp.concatenate([gate_ref[:, span], up_ref[:, span], router_ref[:, span]], axis=0)
        rows = jnp.concatenate([a_ref[d + i, :rows_n, :] for i in range(group)], axis=1)
        total += nt(left, rows)
    for d in range(n_dp):
        term = a_ref[d, rows_n:, :].astype(F32)
        dact += jnp.concatenate([term[:, :rows_n], term[:, rows_n:]], axis=0)
    h, u, logits = total[:units], total[units : 2 * units], total[2 * units :]
    own = jnp.where(iota(logits.shape, 0) == src_ref[0], logits, 0.0)
    gate = jax.nn.sigmoid(jnp.sum(own, axis=0, keepdims=True))
    sig = jax.nn.sigmoid(h)
    act = (h * sig * u).astype(BF16)
    dh = (dact * u * sig * (1.0 + h * (1.0 - sig))).astype(BF16)
    du = (dact * h * sig).astype(BF16)
    dh_ref[...] = dh
    du_ref[...] = du
    dlogit = jnp.sum(act.astype(F32) * dact, axis=0, keepdims=True) * (1.0 - gate)
    lines = [p.astype(F32) for p in pieces(dlogit)]
    extra = c_ref.shape[1] - rows_all
    lines.append(jnp.zeros((extra - len(lines), rows_n), F32))
    lines = jnp.concatenate(lines, axis=0)
    lines = jnp.concatenate([lines, jnp.zeros((extra, cols - rows_n), F32)], axis=1).astype(BF16)
    dht, dut = dh.T, du.T
    for d in range(n_dp):
        span = slice(d * cols, (d + 1) * cols)
        c_ref[d, :rows_n, :] = (nn(dht, gate_ref[:, span]) + nn(dut, up_ref[:, span])).astype(BF16)
        c_ref[d, rows_n:rows_all, :rows_n] = act[:half]
        c_ref[d, rows_n:rows_all, rows_n:] = act[half:]
        c_ref[d, rows_all:, :] = lines


def back_kernel(c_ref, a_ref, down_ref, pick_ref, z_out, r_ref, act_out, z_ref, act_ref, sem):
    n_dp, rows_all, cols = a_ref.shape
    half = act_ref.shape[0] // (2 * n_dp)
    rows_n = rows_all - half
    cap = rows_n // n_dp
    chunks = cols // LANES
    slots = z_ref.shape[0] // n_dp
    diff = jnp.zeros((rows_n, cols), F32)
    packed = jnp.zeros((c_ref.shape[1] - rows_all, cols), F32)
    for d in range(n_dp):
        act_ref[2 * d * half : (2 * d + 1) * half, :] = c_ref[d, rows_n:rows_all, :rows_n]
        act_ref[(2 * d + 1) * half : 2 * (d + 1) * half, :] = c_ref[d, rows_n:rows_all, rows_n:]
        diff += c_ref[d, :rows_n, :].astype(F32)
        packed += c_ref[d, rows_all:, :].astype(F32)
    copies = [pltpu.make_async_copy(act_ref, act_out, sem.at[n_dp])]
    copies[0].start()
    diff = diff.astype(BF16)
    out = tn(act_ref[...], down_ref[...]).astype(BF16)
    for g in range(n_dp):
        own = slice(g * cap, (g + 1) * cap)
        y = jnp.concatenate(
            [
                jnp.concatenate([x[own, c * LANES : (c + 1) * LANES] for x in (out, diff)], axis=1)
                for c in range(chunks)
            ],
            axis=0,
        )
        at = slice(g * slots, (g + 1) * slots)
        z_ref[at, :] = nn(pick_ref[at, :], y).astype(BF16)
        copies.append(pltpu.make_async_copy(z_ref.at[at], z_out.at[at], sem.at[g]))
        copies[-1].start()
    dlogit = packed[:1, :rows_n] + packed[1:2, :rows_n] + packed[2:3, :rows_n]
    terms = [p.astype(F32) for p in pieces(dlogit)]
    terms = jnp.concatenate(terms + [jnp.zeros((8 - len(terms), rows_n), F32)], axis=0).astype(BF16)
    part = r_ref.shape[1]
    lines = []
    for d in range(n_dp):
        line = jnp.sum(nn(terms, a_ref[d, :rows_n, :]), axis=0, keepdims=True)
        lines += [line[:, i : i + part] for i in range(0, cols, part)]
    r_ref[...] = jnp.concatenate(lines, axis=0).astype(BF16)
    for copy in copies:
        copy.wait()


def weight_kernel(dh_ref, du_ref, act_ref, gated_ref, a_ref, gg_ref, ug_ref, dg_ref):
    n_dp, _, cols = a_ref.shape
    rows_n = gated_ref.shape[0]
    dh, du, gated = dh_ref[...], du_ref[...], gated_ref[...]
    for d in range(n_dp):
        span = slice(d * cols, (d + 1) * cols)
        rows = a_ref[d, :rows_n, :]
        gg_ref[:, span] = nn(dh, rows).astype(BF16)
        ug_ref[:, span] = nn(du, rows).astype(BF16)
    step = 256
    for j in range(0, dg_ref.shape[0], step):
        dg_ref[j : j + step, :] = nn(act_ref[j : j + step, :], gated).astype(BF16)


def take_kernel(src_ref, r_ref, *refs):
    far, outs_far, near, near_out, sem = refs[:6], refs[6:9], refs[9:15], refs[15:18], refs[18]
    d_ref, sel_ref, gsel_ref, gates_ref, grad_ref, router_ref = near
    mixed_ref, tgrad_ref, rgrad_ref = near_out
    copies = [pltpu.make_async_copy(a, b, sem.at[i]) for i, (a, b) in enumerate(zip(far, near))]
    for i in (1, 2, 0, 4, 3, 5):
        copies[i].start()
    tok_count, width = grad_ref.shape
    experts = gates_ref.shape[1]
    slots = sel_ref.shape[1]
    n_dp = d_ref.shape[0] // slots
    chunks = slots // (experts * MOST)
    cols = width // n_dp
    back = [
        pltpu.make_async_copy(a, b, sem.at[len(far) + i])
        for i, (a, b) in enumerate(zip(near_out, outs_far))
    ]
    n_rows, part = r_ref.shape
    lines = n_rows // experts
    me = src_ref[0]
    me_x, me_z, me_c = me // 8, (me // 2) % 4, me % 2
    row, col = iota((n_rows, n_rows), 0), iota((n_rows, n_rows), 1)
    block = col // lines
    source = ((me_x + 4 - (block // 2) % 4) % 4) * 8 + ((me_z + 4 - block // 8) % 4) * 2 + (me_c + block) % 2
    sort = ((row % experts == source) & (row // experts == col % lines)).astype(BF16)
    rgrad = nn(sort, r_ref[...])
    for i in range(lines):
        rgrad_ref[:, i * part : (i + 1) * part] = rgrad[i * experts : (i + 1) * experts]
    back[2].start()
    chunk = iota((tok_count, slots), 1) % chunks

    def by_chunk(x):
        return jnp.concatenate(
            [jnp.where(chunk == c, x, jnp.zeros_like(x)) for c in range(chunks)], axis=0
        )

    def span(d, c):
        return slice(d * cols + c * LANES, d * cols + (c + 1) * LANES)

    copies[1].wait()
    copies[2].wait()
    pick = by_chunk(sel_ref[...])
    weights = [by_chunk(w) for w in pieces(gsel_ref[...])]
    copies[0].wait()
    outs = jnp.concatenate([d_ref[d * slots : (d + 1) * slots, :LANES] for d in range(n_dp)], axis=1)
    mixed = sum(nn(w, outs) for w in weights).astype(BF16)
    for d in range(n_dp):
        for c in range(chunks):
            mixed_ref[:, span(d, c)] = mixed[
                c * tok_count : (c + 1) * tok_count, d * LANES : (d + 1) * LANES
            ]
    back[0].start()
    copies[4].wait()
    grads = jnp.concatenate(
        [
            jnp.concatenate([grad_ref[:, span(d, c)] for d in range(n_dp)], axis=1)
            for c in range(chunks)
        ],
        axis=0,
    )
    hits = jnp.where(pick != 0, nt(grads, outs), 0.0)
    hits = sum(hits[c * tok_count : (c + 1) * tok_count] for c in range(chunks))
    collect = (iota((slots, experts), 0) // (MOST * chunks) == iota((slots, experts), 1)).astype(BF16)
    copies[3].wait()
    copies[5].wait()
    gates = gates_ref[...]
    dlogit = sum(nn(p, collect) for p in pieces(hits)) * gates * (1.0 - gates)
    terms = jnp.concatenate(pieces(dlogit), axis=1)
    diffs = jnp.concatenate([d_ref[d * slots : (d + 1) * slots, LANES:] for d in range(n_dp)], axis=1)
    diffs = nn(pick, diffs)
    for d in range(n_dp):
        router = router_ref[:, d * cols : (d + 1) * cols]
        from_router = nn(terms, jnp.concatenate([router] * 3, axis=0))
        for c in range(chunks):
            own = slice(c * tok_count, (c + 1) * tok_count)
            lanes = slice(d * LANES, (d + 1) * LANES)
            tgrad_ref[:, span(d, c)] = (
                diffs[own, lanes] + from_router[:, c * LANES : (c + 1) * LANES]
            ).astype(BF16)
    back[1].start()
    for copy in back:
        copy.wait()


def spread(r):
    def shifted(x, k, to):
        return lax.ppermute(x, "expert", [(e, to(e, k)) for e in range(32)])

    def core(e, k):
        return e // 2 * 2 + (e + k) % 2

    def along_x(e, k):
        return (e + 8 * k) % 32

    def along_z(e, k):
        return e // 8 * 8 + (e + 2 * k) % 8

    for to, n in ((core, 2), (along_x, 4), (along_z, 4)):
        r = jnp.concatenate([r] + [shifted(r, k, to) for k in range(1, n)], axis=0)
    return r


def local(tokens, out_grad, router, choice_index, gate_weight, up_weight, down_weight):
    tok, grad, table = tokens[0], out_grad[0], choice_index[0]
    gate, up, down = gate_weight[0], up_weight[0], down_weight[0]
    router = router.T
    tok_count, width = tok.shape
    experts, cap = table.shape
    units, cols = gate.shape[0], down.shape[1]
    n_dp = lax.axis_size("dp")
    rows_n = n_dp * cap
    chunks = cols // LANES
    per = MOST * chunks
    slots = experts * per
    rows_all = rows_n + units // 2
    src = lax.axis_index("expert").astype(jnp.int32).reshape(1)

    def swap(x, axis):
        return lax.all_to_all(x, axis, split_axis=0, concat_axis=0, tiled=True)

    kept = [((tok_count, slots), BF16), ((tok_count, slots), F32), ((tok_count, experts), F32)]
    x, sel, gsel, gates = call(
        send_kernel,
        [((n_dp, slots, 2 * LANES), BF16)] + kept,
        (src, table, tok, grad, router),
        far_in=(1, 2, 3, 4),
        far_out=(1, 2, 3),
        scratch=[pltpu.VMEM(a.shape, a.dtype) for a in (table, tok, grad, router)]
        + [pltpu.VMEM(s, d) for s, d in kept]
        + [pltpu.SemaphoreType.DMA((4 + len(kept),))],
    )
    x = swap(x.reshape(n_dp * experts, per, 2 * LANES), ("dp", "expert"))
    a, gated, pick = call(
        pack_kernel,
        [
            ((n_dp, rows_all, cols), BF16),
            ((rows_n, cols), BF16),
            ((n_dp * slots, LANES), BF16),
        ],
        (x.reshape(n_dp * slots, 2 * LANES), down),
    )
    a = swap(a, "dp")
    c, dh, du = call(
        hidden_kernel,
        [
            ((n_dp, rows_all + 16, cols), BF16),
            ((units, rows_n), BF16),
            ((units, rows_n), BF16),
        ],
        (src, a, gate, up, router),
    )
    c = swap(c, "dp")
    z, r, act = call(
        back_kernel,
        [
            ((n_dp * slots, 2 * LANES), BF16),
            ((16, width // 16), BF16),
            ((n_dp * units, rows_n), BF16),
        ],
        (c, a, down, pick),
        far_out=(0, 2),
        scratch=[
            pltpu.VMEM((n_dp * slots, 2 * LANES), BF16),
            pltpu.VMEM((n_dp * units, rows_n), BF16),
            pltpu.SemaphoreType.DMA((n_dp + 1,)),
        ],
    )
    z = swap(z.reshape(n_dp * experts, per, 2 * LANES), ("dp", "expert"))
    r = spread(r)
    gate_grad, up_grad, down_grad = call(
        weight_kernel,
        [((units, width), BF16), ((units, width), BF16), ((n_dp * units, cols), BF16)],
        (dh, du, act, gated, a),
    )
    taken = (z.reshape(n_dp * slots, 2 * LANES), sel, gsel, gates, grad, router)
    results = [((tok_count, width), BF16), ((tok_count, width), BF16), ((experts, width), F32)]
    mixed, token_grad, router_grad = call(
        take_kernel,
        results,
        (src, r) + taken,
        far_in=range(2, 8),
        far_out=range(3),
        scratch=[pltpu.VMEM(a.shape, a.dtype) for a in taken]
        + [pltpu.VMEM(s, d) for s, d in results]
        + [pltpu.SemaphoreType.DMA((len(taken) + len(results),))],
    )
    return (
        mixed[None],
        token_grad[None],
        router_grad.T,
        gate_grad[None],
        up_grad[None],
        down_grad[None],
    )


def solution(mesh):
    in_specs = (
        P("dp", "expert", None),
        P("dp", "expert", None),
        P(),
        P("dp", None, None),
        P("expert", "dp", None),
        P("expert", "dp", None),
        P("expert", None, "dp"),
    )
    out_specs = (
        P("dp", "expert", None),
        P("dp", "expert", None),
        P(),
        P("expert", "dp", None),
        P("expert", "dp", None),
        P("expert", None, "dp"),
    )
    return jax.shard_map(local, mesh=mesh, in_specs=in_specs, out_specs=out_specs, check_vma=False)
```

time: 740 us -> 180 us (0.24); the launches traced: 728 us -> 180 us
  waiting for transfers between devices: 457 us -> 12.4 us
  local copies, waits for them, and re-layouts: 57.2 us -> 2.09 us
  blocking collectives: 67.6 us -> 122 us
  other arithmetic: 49.7 us -> 0 us
  matrix products: 36.2 us -> 0 us
  starting transfers between devices: 45.6 us -> 24.5 us
  Pallas kernels: 0 us -> 17.8 us
  between operations: 14.4 us -> 0.91 us
    psum x1 -> x0, waiting for transfers between devices: 226 us -> none  [local(): router_grad = lax.psum(router_terms, ('dp', 'expert'))]
    reduce_scatter x2 -> x0, waiting for transfers between devices: 135 us -> none  [the longest x1 95.9 us: local(): lax.psum_scatter(jnp.einsum('flr,lfd->dlr', hidden_diff, gate_weight, pre...]
    all_to_all x3, blocking collectives: 41.9 us -> 122 us  [swap(): return lax.all_to_all(x, axis, split_axis=0, concat_axis=0, tiled=True)]
    all_gather x1 -> x0, waiting for transfers between devices: 50.9 us -> none  [local(): all_rows = lax.all_gather(expert_rows, 'dp', axis=1, tiled=True)]
    all_to_all x4 -> x1, waiting for transfers between devices: 44.8 us -> 0.01 us  [swap(): return lax.all_to_all(x, axis, split_axis=0, concat_axis=0, tiled=True)]
    unnamed x5 -> x0, other arithmetic: 41.1 us -> none
    dot_general x23 -> x0, matrix products: 36.2 us -> none  [the longest x1 3.06 us: local(): jnp.einsum('emt,emd->td', select, weighted, precision=highest)]
    all_to_all x4 -> x1, starting transfers between devices: 45.1 us -> 9.53 us  [swap(): return lax.all_to_all(x, axis, split_axis=0, concat_axis=0, tiled=True)]
  transfers between devices with their start and end apart: 8 -> 8, of which waited for: 8 -> 6; matrix products, arithmetic and copies ran while one was open for 3% -> 0% of each run, Pallas kernels for 0% -> 2%
where the time goes in v2:
time: 180 us
  blocking collectives  122 us (68%)
  starting transfers between devices  24.5 us (14%)
  Pallas kernels  17.8 us (10%)
  waiting for transfers between devices  12.4 us (7%)
  local copies, waits for them, and re-layouts  2.09 us (1%)
    all_to_all x3, blocking collectives, swap(): return lax.all_to_all(x, axis, split_axis=0, concat_axis=0, tiled=True)  122 us
    pallas_call x6, Pallas kernels, call(): pl.pallas_call(kernel, out_shape=tuple((pltpu.HBM(s, d) if i in far_out e...  17.8 us
    ppermute x7, starting transfers between devices, shifted(): return lax.ppermute(x, 'expert', [(e, to(e, k)) for e in range(32)])  15 us
    ppermute x7, waiting for transfers between devices, shifted(): return lax.ppermute(x, 'expert', [(e, to(e, k)) for e in range(32)])  12.4 us
    all_to_all x1, starting transfers between devices, swap(): return lax.all_to_all(x, axis, split_axis=0, concat_axis=0, tiled=True)  9.53 us
  transfers between devices with their start and end apart: 8, of which 6 were waited for; matrix products, arithmetic and copies ran while one was open for 0% of the time, Pallas kernels for 2%

profile of v2, /device:TPU:1, one launch (start us, length us, event | category | flops | bytes accessed | tf_op | source)
XLA Modules:
  0.0 180.0 jit_solution(17943333125012991677)
XLA Ops:
  0.6 2.9 %shard_map.118 = (bf16[8,256,256]{2,1,0:T(8,128)(2,1)S(1)}, bf16[64,256]{1,0:T(8,128)(2,1)}, f32[64,256]{1,0:T(8,128)}, f32[64,32]{1,0:T(8,128)}) custom-call(s32[1]{0:T(128)} %bitcast.src_ref, s32[32,32]{1,0:T(8,128)} %bitcast.31, bf16[64,4096]{1,0:T(8,128)(2,1)} %bitcast.30, bf16[64,4096]{1,0:T(8,128)(2,1)} %bitcast.27, bf16[32,4096]{1,0:T(8,128)(2,1)} %bitcast.21), custom_call_target="tpu_custom_call" | custom-call | tf_op jit(solution)/shard_map/pallas_call | solution.py:46
  3.5 46.6 %all_to_all.20 = bf16[256,8,256]{2,1,0:T(8,128)(2,1)S(1)} all-to-all(bf16[256,8,256]{2,1,0:T(8,128)(2,1)S(1)} %bitcast.26), channel_id=1, replica_groups=mesh['dp'=8,'expert'=32] {'dp','expert'}, dimensions={0} | all-to-all | bytes 2097152 | tf_op jit(solution)/shard_map/all_to_all | solution.py:376
  50.2 1.7 shard_map.119
  51.9 0.0 copy-start.1
  51.9 0.0 copy-start.2
  51.9 0.0 copy-start.3
  51.9 37.9 %all_to_all.21.a_ref = bf16[8,352,512]{2,1,0:T(8,128)(2,1)S(1)} all-to-all(bf16[8,352,512]{2,1,0:T(8,128)(2,1)S(1)} %get-tuple-element.26), channel_id=1, replica_groups=mesh['dp'=8,'expert'=32] {'dp'}, dimensions={0} | all-to-all | bytes 5767168 | tf_op jit(solution)/shard_map/all_to_all | solution.py:376
  89.8 0.0 copy-done.3
  89.8 4.0 %shard_map.120 = (bf16[8,368,512]{2,1,0:T(8,128)(2,1)S(1)}, bf16[192,256]{1,0:T(8,128)(2,1)S(1)}, bf16[192,256]{1,0:T(8,128)(2,1)S(1)}) custom-call(s32[1]{0:T(128)} %bitcast.src_ref, bf16[8,352,512]{2,1,0:T(8,128)(2,1)S(1)} %all_to_all.21.a_ref, bf16[192,4096]{1,0:T(8,128)(2,1)S(1)} %bitcast.24, bf16[192,4096]{1,0:T(8,128)(2,1)S(1)} %bitcast.25, ...), custom_call_target="tpu_custom_call" | custom-call | tf_op jit(solution)/shard_map/pallas_call | solution.py:46
  93.9 0.0 copy-start.5
  93.9 37.7 %all_to_all.22.c_ref = bf16[8,368,512]{2,1,0:T(8,128)(2,1)S(1)} all-to-all(bf16[8,368,512]{2,1,0:T(8,128)(2,1)S(1)} %get-tuple-element.27), channel_id=1, replica_groups=mesh['dp'=8,'expert'=32] {'dp'}, dimensions={0} | all-to-all | bytes 6029312 | tf_op jit(solution)/shard_map/all_to_all | solution.py:376
  131.6 1.8 %shard_map.121 = (bf16[2048,256]{1,0:T(8,128)(2,1)}, bf16[16,256]{1,0:T(8,128)(2,1)S(1)}, bf16[1536,256]{1,0:T(8,128)(2,1)}) custom-call(bf16[8,368,512]{2,1,0:T(8,128)(2,1)S(1)} %all_to_all.22.c_ref, bf16[8,352,512]{2,1,0:T(8,128)(2,1)S(1)} %all_to_all.21.a_ref, bf16[1536,512]{1,0:T(8,128)(2,1)S(1)} %bitcast.19, ...), custom_call_target="tpu_custom_call" | custom-call | tf_op jit(solution)/shard_map/pallas_call | solution.py:46
  133.4 9.5 %all-to-all-start.3 = ((bf16[256,8,256]{2,1,0:T(8,128)(2,1)}), bf16[256,8,256]{2,1,0:T(8,128)(2,1)}, u32[]{:S(2)}, u32[]{:S(2)}) async-start(bf16[256,8,256]{2,1,0:T(8,128)(2,1)} %bitcast.29), calls=%async_computation.3 | async-start | bytes 2097152 | tf_op jit(solution)/shard_map/all_to_all | solution.py:376
  143.0 2.3 %collective-permute-start = (bf16[16,256]{1,0:T(8,128)(2,1)S(1)}, bf16[16,256]{1,0:T(8,128)(2,1)S(1)}, u32[]{:S(2)}, u32[]{:S(2)}) collective-permute-start(bf16[16,256]{1,0:T(8,128)(2,1)S(1)} %get-tuple-element.29), channel_id=1, source_target_pairs={{0,1},{1,0},{2,3},{3,2},{4,5},{5,4},{6,7},{7,6},{8,9},{9,8},{10,11... | collective-permute-start | bytes 24584 | tf_op jit(solution)/shard_map/ppermute | solution.py:344
  145.3 0.8 collective-permute-done
  146.1 0.0 collective-permute-start.1
  146.1 1.9 %collective-permute-start.2 = (bf16[32,256]{1,0:T(8,128)(2,1)S(1)}, bf16[32,256]{1,0:T(8,128)(2,1)S(1)}, u32[]{:S(2)}, u32[]{:S(2)}) collective-permute-start(bf16[32,256]{1,0:T(8,128)(2,1)S(1)} %get-tuple-element.52), channel_id=1, source_target_pairs={{0,16},{1,17},{2,18},{3,19},{4,20},{5,21},{6,22},{7,23},{8,24},{9,... | collective-permute-start | bytes 49160 | tf_op jit(solution)/shard_map/ppermute | solution.py:344
  148.0 1.2 collective-permute-start.3
  149.2 1.1 collective-permute-done.1
  150.3 0.6 collective-permute-done.2
  151.0 0.3 collective-permute-done.3
  151.3 2.3 %collective-permute-start.4 = (bf16[128,256]{1,0:T(8,128)(2,1)S(1)}, bf16[128,256]{1,0:T(8,128)(2,1)S(1)}, u32[]{:S(2)}, u32[]{:S(2)}) collective-permute-start(bf16[128,256]{1,0:T(8,128)(2,1)S(1)} %get-tuple-element.44), channel_id=1, source_target_pairs={{0,2},{1,3},{2,4},{3,5},{4,6},{5,7},{6,0},{7,1},{8,10},{9,11},{10,... | collective-permute-start | bytes 196616 | tf_op jit(solution)/shard_map/ppermute | solution.py:344
  153.6 1.1 copy-done.4
  154.7 0.9 copy-done.6
  155.6 3.1 %shard_map.123 = (bf16[192,4096]{1,0:T(8,128)(2,1)}, bf16[192,4096]{1,0:T(8,128)(2,1)}, bf16[1536,512]{1,0:T(8,128)(2,1)}) custom-call(bf16[192,256]{1,0:T(8,128)(2,1)S(1)} %get-tuple-element.37.dh_ref, bf16[192,256]{1,0:T(8,128)(2,1)S(1)} %copy-done.6, bf16[1536,256]{1,0:T(8,128)(2,1)S(1)} %copy-done.4, bf16[256,512]{1,0:T(8,128)(2,1)S(1)} %get-tuple-element.40.gated_ref, ...), custom_call_target="tpu_custom_call" | custom-call | tf_op jit(solution)/shard_map/pallas_call | solution.py:46
  158.7 4.6 %collective-permute-start.5 = (bf16[128,256]{1,0:T(8,128)(2,1)S(1)}, bf16[128,256]{1,0:T(8,128)(2,1)S(1)}, u32[]{:S(2)}, u32[]{:S(2)}) collective-permute-start(bf16[128,256]{1,0:T(8,128)(2,1)S(1)} %get-tuple-element.44), channel_id=1, source_target_pairs={{0,4},{1,5},{2,6},{3,7},{4,0},{5,1},{6,2},{7,3},{8,12},{9,13},{10,... | collective-permute-start | bytes 196616 | tf_op jit(solution)/shard_map/ppermute | solution.py:344
  163.3 2.7 %collective-permute-start.6 = (bf16[128,256]{1,0:T(8,128)(2,1)S(1)}, bf16[128,256]{1,0:T(8,128)(2,1)S(1)}, u32[]{:S(2)}, u32[]{:S(2)}) collective-permute-start(bf16[128,256]{1,0:T(8,128)(2,1)S(1)} %get-tuple-element.44), channel_id=1, source_target_pairs={{0,6},{1,7},{2,0},{3,1},{4,2},{5,3},{6,4},{7,5},{8,14},{9,15},{10,... | collective-permute-start | bytes 196616 | tf_op jit(solution)/shard_map/ppermute | solution.py:344
  166.0 4.4 %collective-permute-done.4 = bf16[128,256]{1,0:T(8,128)(2,1)S(1)} collective-permute-done((bf16[128,256]{1,0:T(8,128)(2,1)S(1)}, bf16[128,256]{1,0:T(8,128)(2,1)S(1)}, u32[]{:S(2)}, u32[]{:S(2)}) %collective-permute-start.4) | collective-permute-done | bytes 65568 | tf_op jit(solution)/shard_map/ppermute | solution.py:344
  170.4 5.1 %collective-permute-done.5 = bf16[128,256]{1,0:T(8,128)(2,1)S(1)} collective-permute-done((bf16[128,256]{1,0:T(8,128)(2,1)S(1)}, bf16[128,256]{1,0:T(8,128)(2,1)S(1)}, u32[]{:S(2)}, u32[]{:S(2)}) %collective-permute-start.5) | collective-permute-done | bytes 65568 | tf_op jit(solution)/shard_map/ppermute | solution.py:344
  175.5 0.0 collective-permute-done.6
  175.5 0.0 all-to-all-done.3
  175.5 4.3 %shard_map.122 = (bf16[64,4096]{1,0:T(8,128)(2,1)}, bf16[64,4096]{1,0:T(8,128)(2,1)}, f32[32,4096]{1,0:T(8,128)}) custom-call(s32[1]{0:T(128)} %bitcast.src_ref, bf16[512,256]{1,0:T(8,128)(2,1)S(1)} %constant_dynamic-update-slice_fusion.7.r_ref, bf16[2048,256]{1,0:T(8,128)(2,1)} %bitcast.11.refs_0_, bf16[64,256]{1,0:T(8,128)(2,1)} %get-tuple-element.31.refs_1_, ...), custom_call_target="tpu_custom_call" | custom-call | tf_op jit(solution)/shard_map/pallas_call | solution.py:46
  (15 shorter events, 0.0 us)
Async XLA Ops:
  0.6 49.5 %copy-start = (bf16[1,1536,512]{2,1,0:T(8,128)(2,1)S(1)}, bf16[1,1536,512]{2,1,0:T(8,128)(2,1)}, u32[]{:S(2)}) copy-start(bf16[1,1536,512]{2,1,0:T(8,128)(2,1)} %param.13) | copy-start | bytes 4718596
  51.9 37.9 %copy-start.1 = (bf16[4096,32]{0,1:T(8,128)(2,1)S(1)}, bf16[4096,32]{0,1:T(8,128)(2,1)}, u32[]{:S(2)}) copy-start(bf16[4096,32]{0,1:T(8,128)(2,1)} %param.9) | copy-start | bytes 786436
  51.9 37.9 %copy-start.2 = (bf16[1,192,4096]{2,1,0:T(8,128)(2,1)S(1)}, bf16[1,192,4096]{2,1,0:T(8,128)(2,1)}, u32[]{:S(2)}) copy-start(bf16[1,192,4096]{2,1,0:T(8,128)(2,1)} %param.11) | copy-start | bytes 4718596
  51.9 37.9 %copy-start.3 = (bf16[1,192,4096]{2,1,0:T(8,128)(2,1)S(1)}, bf16[1,192,4096]{2,1,0:T(8,128)(2,1)}, u32[]{:S(2)}) copy-start(bf16[1,192,4096]{2,1,0:T(8,128)(2,1)} %param.12) | copy-start | bytes 4718596
  93.9 37.7 %copy-start.5 = (bf16[192,256]{1,0:T(8,128)(2,1)}, bf16[192,256]{1,0:T(8,128)(2,1)S(1)}, u32[]{:S(2)}) copy-start(bf16[192,256]{1,0:T(8,128)(2,1)S(1)} %get-tuple-element.38.du_ref) | copy-start | bytes 294916
  133.4 42.1 %all-to-all-start.3 = ((bf16[256,8,256]{2,1,0:T(8,128)(2,1)}), bf16[256,8,256]{2,1,0:T(8,128)(2,1)}, u32[]{:S(2)}, u32[]{:S(2)}) async-start(bf16[256,8,256]{2,1,0:T(8,128)(2,1)} %bitcast.29), calls=%async_computation.3 | async-start | bytes 2097152 | tf_op jit(solution)/shard_map/all_to_all | solution.py:376
  143.0 3.1 %collective-permute-start = (bf16[16,256]{1,0:T(8,128)(2,1)S(1)}, bf16[16,256]{1,0:T(8,128)(2,1)S(1)}, u32[]{:S(2)}, u32[]{:S(2)}) collective-permute-start(bf16[16,256]{1,0:T(8,128)(2,1)S(1)} %get-tuple-element.29), channel_id=1, source_target_pairs={{0,1},{1,0},{2,3},{3,2},{4,5},{5,4},{6,7},{7,6},{8,9},{9,8},{10,11... | collective-permute-start | bytes 24584 | tf_op jit(solution)/shard_map/ppermute | solution.py:344
  146.1 4.2 %collective-permute-start.1 = (bf16[32,256]{1,0:T(8,128)(2,1)S(1)}, bf16[32,256]{1,0:T(8,128)(2,1)S(1)}, u32[]{:S(2)}, u32[]{:S(2)}) collective-permute-start(bf16[32,256]{1,0:T(8,128)(2,1)S(1)} %get-tuple-element.52), channel_id=1, source_target_pairs={{0,8},{1,9},{2,10},{3,11},{4,12},{5,13},{6,14},{7,15},{8,16},{9,17... | collective-permute-start | bytes 49160 | tf_op jit(solution)/shard_map/ppermute | solution.py:344
  146.1 4.9 %collective-permute-start.2 = (bf16[32,256]{1,0:T(8,128)(2,1)S(1)}, bf16[32,256]{1,0:T(8,128)(2,1)S(1)}, u32[]{:S(2)}, u32[]{:S(2)}) collective-permute-start(bf16[32,256]{1,0:T(8,128)(2,1)S(1)} %get-tuple-element.52), channel_id=1, source_target_pairs={{0,16},{1,17},{2,18},{3,19},{4,20},{5,21},{6,22},{7,23},{8,24},{9,... | collective-permute-start | bytes 49160 | tf_op jit(solution)/shard_map/ppermute | solution.py:344
  148.0 3.3 %collective-permute-start.3 = (bf16[32,256]{1,0:T(8,128)(2,1)S(1)}, bf16[32,256]{1,0:T(8,128)(2,1)S(1)}, u32[]{:S(2)}, u32[]{:S(2)}) collective-permute-start(bf16[32,256]{1,0:T(8,128)(2,1)S(1)} %get-tuple-element.52), channel_id=1, source_target_pairs={{0,24},{1,25},{2,26},{3,27},{4,28},{5,29},{6,30},{7,31},{8,0},{9,1... | collective-permute-start | bytes 49160 | tf_op jit(solution)/shard_map/ppermute | solution.py:344
  151.3 19.1 %collective-permute-start.4 = (bf16[128,256]{1,0:T(8,128)(2,1)S(1)}, bf16[128,256]{1,0:T(8,128)(2,1)S(1)}, u32[]{:S(2)}, u32[]{:S(2)}) collective-permute-start(bf16[128,256]{1,0:T(8,128)(2,1)S(1)} %get-tuple-element.44), channel_id=1, source_target_pairs={{0,2},{1,3},{2,4},{3,5},{4,6},{5,7},{6,0},{7,1},{8,10},{9,11},{10,... | collective-permute-start | bytes 196616 | tf_op jit(solution)/shard_map/ppermute | solution.py:344
  153.6 1.1 copy-start.4
  154.7 0.9 copy-start.6
  158.7 16.7 %collective-permute-start.5 = (bf16[128,256]{1,0:T(8,128)(2,1)S(1)}, bf16[128,256]{1,0:T(8,128)(2,1)S(1)}, u32[]{:S(2)}, u32[]{:S(2)}) collective-permute-start(bf16[128,256]{1,0:T(8,128)(2,1)S(1)} %get-tuple-element.44), channel_id=1, source_target_pairs={{0,4},{1,5},{2,6},{3,7},{4,0},{5,1},{6,2},{7,3},{8,12},{9,13},{10,... | collective-permute-start | bytes 196616 | tf_op jit(solution)/shard_map/ppermute | solution.py:344
  163.3 12.2 %collective-permute-start.6 = (bf16[128,256]{1,0:T(8,128)(2,1)S(1)}, bf16[128,256]{1,0:T(8,128)(2,1)S(1)}, u32[]{:S(2)}, u32[]{:S(2)}) collective-permute-start(bf16[128,256]{1,0:T(8,128)(2,1)S(1)} %get-tuple-element.44), channel_id=1, source_target_pairs={{0,6},{1,7},{2,0},{3,1},{4,2},{5,3},{6,4},{7,5},{8,14},{9,15},{10,... | collective-permute-start | bytes 196616 | tf_op jit(solution)/shard_map/ppermute | solution.py:344

commit v3 on v2

--- a/solution.py
+++ b/solution.py
@@ -56,23 +56,39 @@
     )(*args)
 
 
+def chunked(src, dst, n, sem, at):
+    rows = src.shape[0] // n
+    parts = [pl.ds(i * rows, rows) for i in range(n)]
+    return [pltpu.make_async_copy(src.at[p], dst.at[p], sem.at[at + i]) for i, p in enumerate(parts)]
+
+
+def start(copies):
+    for copy in copies:
+        copy.start()
+
+
+def wait(copies):
+    for copy in copies:
+        copy.wait()
+
+
 def send_kernel(src_ref, *refs):
     far, x_ref, outs_far, near, near_out, sem = refs[:4], refs[4], refs[5:8], refs[8:12], refs[12:15], refs[15]
     sel_ref, gsel_ref, gates_ref = near_out
-    back = [
-        pltpu.make_async_copy(a, b, sem.at[len(far) + i])
-        for i, (a, b) in enumerate(zip(near_out, outs_far))
-    ]
-    copies = [pltpu.make_async_copy(a, b, sem.at[i]) for i, (a, b) in enumerate(zip(far, near))]
-    for copy in copies:
-        copy.start()
+    copies, at = [], 0
+    for src, dst, n in zip(far, near, (1, 4, 4, 2)):
+        copies.append(chunked(src, dst, n, sem, at))
+        at += n
+    back = [pltpu.make_async_copy(a, b, sem.at[at + i]) for i, (a, b) in enumerate(zip(near_out, outs_far))]
+    for i in (0, 3, 1, 2):
+        start(copies[i])
     table_ref, tok_ref, grad_ref, router_ref = near
     tok_count, width = tok_ref.shape
     experts, cap = table_ref.shape
     n_dp, slots, _ = x_ref.shape
     chunks = slots // (experts * MOST)
     cols = width // n_dp
-    copies[0].wait()
+    wait(copies[0])
     table = table_ref[...]
     owner = table // tok_count
     offset = table - owner * tok_count
@@ -91,8 +107,8 @@
             jnp.where(own_col & (col_rank == m), chosen, 0.0), axis=0, keepdims=True
         )
     sel = (iota((tok_count, slots), 0) + 1).astype(F32) == wanted
-    copies[3].wait()
-    copies[1].wait()
+    wait(copies[3])
+    wait(copies[1])
     gates = jax.nn.sigmoid(nt(tok_ref[...], router_ref[...]))
     gates_ref[...] = gates
     expand = own_col.astype(BF16)
@@ -101,8 +117,7 @@
     sel_low = sel.astype(BF16)
     sel_ref[...] = sel_low
     gsel_ref[...] = gsel
-    for copy in back:
-        copy.start()
+    start(back)
     ones = jnp.ones((tok_count, LANES), BF16)
     slot_gate = sum(tn(p, ones) for p in pieces(gsel))
     slot_empty = (1.0 - tn(sel_low, ones)) * EMPTY
@@ -110,7 +125,7 @@
     pick = jnp.concatenate(
         [jnp.where(chunk == c, sel_low, jnp.zeros_like(sel_low)) for c in range(chunks)], axis=0
     )
-    copies[2].wait()
+    wait(copies[2])
     for d in range(n_dp):
         parts = []
         for c in range(chunks):
@@ -119,8 +134,7 @@
         got = tn(pick, jnp.concatenate(parts, axis=0))
         x_ref[d, :, :LANES] = (got[:, :LANES] + slot_empty).astype(BF16)
         x_ref[d, :, LANES:] = (got[:, LANES:] * slot_gate).astype(BF16)
-    for copy in back:
-        copy.wait()
+    wait(back)
 
 
 def pack_kernel(x_ref, down_ref, p_ref, gated_ref, pick_ref):
@@ -156,7 +170,7 @@
         p_ref[d, rows_n:, rows_n:] = term[half:]
 
 
-def hidden_kernel(src_ref, a_ref, gate_ref, up_ref, router_ref, c_ref, dh_ref, du_ref):
+def hidden_kernel(src_ref, a_ref, gate_ref, up_ref, router_ref, dh_ref, du_ref, act_ref, lines_ref):
     units, width = gate_ref.shape
     experts = router_ref.shape[0]
     n_dp, rows_all, cols = a_ref.shape
@@ -184,11 +198,20 @@
     du_ref[...] = du
     dlogit = jnp.sum(act.astype(F32) * dact, axis=0, keepdims=True) * (1.0 - gate)
     lines = [p.astype(F32) for p in pieces(dlogit)]
-    extra = c_ref.shape[1] - rows_all
+    extra = lines_ref.shape[0]
     lines.append(jnp.zeros((extra - len(lines), rows_n), F32))
     lines = jnp.concatenate(lines, axis=0)
-    lines = jnp.concatenate([lines, jnp.zeros((extra, cols - rows_n), F32)], axis=1).astype(BF16)
-    dht, dut = dh.T, du.T
+    lines_ref[...] = jnp.concatenate([lines, jnp.zeros((extra, cols - rows_n), F32)], axis=1).astype(BF16)
+    act_ref[...] = act
+
+
+def diff_kernel(dh_ref, du_ref, act_ref, lines_ref, gate_ref, up_ref, c_ref):
+    units, rows_n = act_ref.shape
+    n_dp, _, cols = c_ref.shape
+    half = units // 2
+    rows_all = rows_n + half
+    act, lines = act_ref[...], lines_ref[...]
+    dht, dut = dh_ref[...].T, du_ref[...].T
     for d in range(n_dp):
         span = slice(d * cols, (d + 1) * cols)
         c_ref[d, :rows_n, :] = (nn(dht, gate_ref[:, span]) + nn(dut, up_ref[:, span])).astype(BF16)
@@ -259,19 +282,70 @@
     far, outs_far, near, near_out, sem = refs[:6], refs[6:9], refs[9:15], refs[15:18], refs[18]
     d_ref, sel_ref, gsel_ref, gates_ref, grad_ref, router_ref = near
     mixed_ref, tgrad_ref, rgrad_ref = near_out
-    copies = [pltpu.make_async_copy(a, b, sem.at[i]) for i, (a, b) in enumerate(zip(far, near))]
+    copies, at = [], 0
+    for a, b, n in zip(far, near, (4, 1, 1, 1, 1, 1)):
+        copies.append(chunked(a, b, n, sem, at))
+        at += n
     for i in (1, 2, 0, 4, 3, 5):
-        copies[i].start()
+        start(copies[i])
     tok_count, width = grad_ref.shape
     experts = gates_ref.shape[1]
     slots = sel_ref.shape[1]
     n_dp = d_ref.shape[0] // slots
     chunks = slots // (experts * MOST)
     cols = width // n_dp
-    back = [
-        pltpu.make_async_copy(a, b, sem.at[len(far) + i])
-        for i, (a, b) in enumerate(zip(near_out, outs_far))
-    ]
+    rgrad_back = chunked(rgrad_ref, outs_far[2], 1, sem, at)
+    at += 1
+
+    def column_copies(i, at):
+        blocks = [pl.ds(d * cols, 2 * cols) for d in range(0, n_dp, 2)]
+        return [
+            pltpu.make_async_copy(near_out[i].at[:, b], outs_far[i].at[:, b], sem.at[at + d])
+            for d, b in enumerate(blocks)
+        ]
+
+    mixed_back = column_copies(0, at)
+    tgrad_back = column_copies(1, at + n_dp)
+    chunk = iota((tok_count, slots), 1) % chunks
+
+    def by_chunk(x):
+        return jnp.concatenate(
+            [jnp.where(chunk == c, x, jnp.zeros_like(x)) for c in range(chunks)], axis=0
+        )
+
+    def span(d, c):
+        return slice(d * cols + c * LANES, d * cols + (c + 1) * LANES)
+
+    def both(d, lanes):
+        return jnp.concatenate(
+            [d_ref[i * slots : (i + 1) * slots, lanes] for i in (d, d + 1)], axis=1
+        )
+
+    wait(copies[1])
+    wait(copies[2])
+    pick = by_chunk(sel_ref[...])
+    weights = [by_chunk(w) for w in pieces(gsel_ref[...])]
+    hits = jnp.zeros(pick.shape, F32)
+    for d in range(0, n_dp, 2):
+        wait(copies[0][d // 2 : d // 2 + 1])
+        outs = both(d, slice(0, LANES))
+        mixed = sum(nn(w, outs) for w in weights).astype(BF16)
+        for i in range(2):
+            for c in range(chunks):
+                mixed_ref[:, span(d + i, c)] = mixed[
+                    c * tok_count : (c + 1) * tok_count, i * LANES : (i + 1) * LANES
+                ]
+        mixed_back[d // 2].start()
+        if d == 0:
+            wait(copies[4])
+        grads = jnp.concatenate(
+            [
+                jnp.concatenate([grad_ref[:, span(d + i, c)] for i in range(2)], axis=1)
+                for c in range(chunks)
+            ],
+            axis=0,
+        )
+        hits += nt(grads, outs)
     n_rows, part = r_ref.shape
     lines = n_rows // experts
     me = src_ref[0]
@@ -283,60 +357,30 @@
     rgrad = nn(sort, r_ref[...])
     for i in range(lines):
         rgrad_ref[:, i * part : (i + 1) * part] = rgrad[i * experts : (i + 1) * experts]
-    back[2].start()
-    chunk = iota((tok_count, slots), 1) % chunks
-
-    def by_chunk(x):
-        return jnp.concatenate(
-            [jnp.where(chunk == c, x, jnp.zeros_like(x)) for c in range(chunks)], axis=0
-        )
-
-    def span(d, c):
-        return slice(d * cols + c * LANES, d * cols + (c + 1) * LANES)
-
-    copies[1].wait()
-    copies[2].wait()
-    pick = by_chunk(sel_ref[...])
-    weights = [by_chunk(w) for w in pieces(gsel_ref[...])]
-    copies[0].wait()
-    outs = jnp.concatenate([d_ref[d * slots : (d + 1) * slots, :LANES] for d in range(n_dp)], axis=1)
-    mixed = sum(nn(w, outs) for w in weights).astype(BF16)
-    for d in range(n_dp):
-        for c in range(chunks):
-            mixed_ref[:, span(d, c)] = mixed[
-                c * tok_count : (c + 1) * tok_count, d * LANES : (d + 1) * LANES
-            ]
-    back[0].start()
-    copies[4].wait()
-    grads = jnp.concatenate(
-        [
-            jnp.concatenate([grad_ref[:, span(d, c)] for d in range(n_dp)], axis=1)
-            for c in range(chunks)
-        ],
-        axis=0,
-    )
-    hits = jnp.where(pick != 0, nt(grads, outs), 0.0)
+    start(rgrad_back)
+    hits = jnp.where(pick != 0, hits, 0.0)
     hits = sum(hits[c * tok_count : (c + 1) * tok_count] for c in range(chunks))
     collect = (iota((slots, experts), 0) // (MOST * chunks) == iota((slots, experts), 1)).astype(BF16)
-    copies[3].wait()
-    copies[5].wait()
+    wait(copies[3])
+    wait(copies[5])
     gates = gates_ref[...]
     dlogit = sum(nn(p, collect) for p in pieces(hits)) * gates * (1.0 - gates)
     terms = jnp.concatenate(pieces(dlogit), axis=1)
-    diffs = jnp.concatenate([d_ref[d * slots : (d + 1) * slots, LANES:] for d in range(n_dp)], axis=1)
-    diffs = nn(pick, diffs)
-    for d in range(n_dp):
-        router = router_ref[:, d * cols : (d + 1) * cols]
+    for d in range(0, n_dp, 2):
+        diffs = nn(pick, both(d, slice(LANES, 2 * LANES)))
+        router = router_ref[:, d * cols : (d + 2) * cols]
         from_router = nn(terms, jnp.concatenate([router] * 3, axis=0))
-        for c in range(chunks):
-            own = slice(c * tok_count, (c + 1) * tok_count)
-            lanes = slice(d * LANES, (d + 1) * LANES)
-            tgrad_ref[:, span(d, c)] = (
-                diffs[own, lanes] + from_router[:, c * LANES : (c + 1) * LANES]
-            ).astype(BF16)
-    back[1].start()
-    for copy in back:
-        copy.wait()
+        for i in range(2):
+            for c in range(chunks):
+                at = i * cols + c * LANES
+                tgrad_ref[:, span(d + i, c)] = (
+                    diffs[c * tok_count : (c + 1) * tok_count, i * LANES : (i + 1) * LANES]
+                    + from_router[:, at : at + LANES]
+                ).astype(BF16)
+        tgrad_back[d // 2].start()
+    wait(rgrad_back)
+    wait(mixed_back)
+    wait(tgrad_back)
 
 
 def spread(r):
@@ -353,8 +397,9 @@
         return e // 8 * 8 + (e + 2 * k) % 8
 
     for to, n in ((core, 2), (along_x, 4), (along_z, 4)):
+        half = r
         r = jnp.concatenate([r] + [shifted(r, k, to) for k in range(1, n)], axis=0)
-    return r
+    return r, half
 
 
 def local(tokens, out_grad, router, choice_index, gate_weight, up_weight, down_weight):
@@ -384,7 +429,7 @@
         far_out=(1, 2, 3),
         scratch=[pltpu.VMEM(a.shape, a.dtype) for a in (table, tok, grad, router)]
         + [pltpu.VMEM(s, d) for s, d in kept]
-        + [pltpu.SemaphoreType.DMA((4 + len(kept),))],
+        + [pltpu.SemaphoreType.DMA((11 + len(kept),))],
     )
     x = swap(x.reshape(n_dp * experts, per, 2 * LANES), ("dp", "expert"))
     a, gated, pick = call(
@@ -397,14 +442,13 @@
         (x.reshape(n_dp * slots, 2 * LANES), down),
     )
     a = swap(a, "dp")
-    c, dh, du = call(
+    dh, du, act, lines = call(
         hidden_kernel,
-        [
-            ((n_dp, rows_all + 16, cols), BF16),
-            ((units, rows_n), BF16),
-            ((units, rows_n), BF16),
-        ],
+        [((units, rows_n), BF16)] * 3 + [((16, cols), BF16)],
         (src, a, gate, up, router),
+    )
+    (c,) = call(
+        diff_kernel, [((n_dp, rows_all + 16, cols), BF16)], (dh, du, act, lines, gate, up)
     )
     c = swap(c, "dp")
     z, r, act = call(
@@ -423,7 +467,8 @@
         ],
     )
     z = swap(z.reshape(n_dp * experts, per, 2 * LANES), ("dp", "expert"))
-    r = spread(r)
+    r, half = spread(r)
+    dh, half = lax.optimization_barrier((dh, half))
     gate_grad, up_grad, down_grad = call(
         weight_kernel,
         [((units, width), BF16), ((units, width), BF16), ((n_dp * units, cols), BF16)],
@@ -439,7 +484,7 @@
         far_out=range(3),
         scratch=[pltpu.VMEM(a.shape, a.dtype) for a in taken]
         + [pltpu.VMEM(s, d) for s, d in results]
-        + [pltpu.SemaphoreType.DMA((len(taken) + len(results),))],
+        + [pltpu.SemaphoreType.DMA((21 + 2 * n_dp,))],
     )
     return (
         mixed[None],

time: 180 us -> 179 us (level)
    pallas_call x6 -> x7, Pallas kernels: 17.8 us -> 16.2 us  [call(): pl.pallas_call(kernel, out_shape=tuple((pltpu.HBM(s, d) if i in far_out e...]
where the time goes in v3:
time: 179 us; the launch traced here: 178 us
  blocking collectives  122 us (68%)
  starting transfers between devices  24.5 us (14%)
  Pallas kernels  16.2 us (9%)
  waiting for transfers between devices  12.3 us (7%)
  local copies, waits for them, and re-layouts  2.14 us (1%)
    all_to_all x3, blocking collectives, swap(): return lax.all_to_all(x, axis, split_axis=0, concat_axis=0, tiled=True)  122 us
    pallas_call x7, Pallas kernels, call(): pl.pallas_call(kernel, out_shape=tuple((pltpu.HBM(s, d) if i in far_out e...  16.2 us
    ppermute x7, starting transfers between devices, shifted(): return lax.ppermute(x, 'expert', [(e, to(e, k)) for e in range(32)])  15 us
    ppermute x7, waiting for transfers between devices, shifted(): return lax.ppermute(x, 'expert', [(e, to(e, k)) for e in range(32)])  12.3 us
    all_to_all x1, starting transfers between devices, swap(): return lax.all_to_all(x, axis, split_axis=0, concat_axis=0, tiled=True)  9.54 us
  transfers between devices with their start and end apart: 8, of which 6 were waited for; matrix products, arithmetic and copies ran while one was open for 0% of the time, Pallas kernels for 2%

profile of v3, /device:TPU:1, one launch (start us, length us, event | category | flops | bytes accessed | tf_op | source)
XLA Modules:
  0.0 178.4 jit_solution(5939672553029206095)
XLA Ops:
  0.6 2.8 %shard_map.118 = (bf16[8,256,256]{2,1,0:T(8,128)(2,1)S(1)}, bf16[64,256]{1,0:T(8,128)(2,1)}, f32[64,256]{1,0:T(8,128)}, f32[64,32]{1,0:T(8,128)}) custom-call(s32[1]{0:T(128)} %bitcast.src_ref, s32[32,32]{1,0:T(8,128)} %bitcast.33, bf16[64,4096]{1,0:T(8,128)(2,1)} %bitcast.32, bf16[64,4096]{1,0:T(8,128)(2,1)} %bitcast.29, bf16[32,4096]{1,0:T(8,128)(2,1)} %bitcast.25), custom_call_target="tpu_custom_call" | custom-call | tf_op jit(solution)/shard_map/pallas_call | solution.py:46
  3.5 46.6 %all_to_all.20 = bf16[256,8,256]{2,1,0:T(8,128)(2,1)S(1)} all-to-all(bf16[256,8,256]{2,1,0:T(8,128)(2,1)S(1)} %bitcast.28), channel_id=1, replica_groups=mesh['dp'=8,'expert'=32] {'dp','expert'}, dimensions={0} | all-to-all | bytes 2097152 | tf_op jit(solution)/shard_map/all_to_all | solution.py:421
  50.1 1.7 shard_map.119
  51.9 0.0 copy-start.5
  51.9 0.0 copy-start
  51.9 0.0 copy-start.1
  51.9 0.0 copy-start.3
  51.9 37.9 %all_to_all.21.a_ref = bf16[8,352,512]{2,1,0:T(8,128)(2,1)S(1)} all-to-all(bf16[8,352,512]{2,1,0:T(8,128)(2,1)S(1)} %get-tuple-element.28), channel_id=1, replica_groups=mesh['dp'=8,'expert'=32] {'dp'}, dimensions={0} | all-to-all | bytes 5767168 | tf_op jit(solution)/shard_map/all_to_all | solution.py:421
  89.9 1.2 shard_map.120
  91.0 1.3 shard_map.121
  92.3 37.7 %all_to_all.22.c_ref = bf16[8,368,512]{2,1,0:T(8,128)(2,1)S(1)} all-to-all(bf16[8,368,512]{2,1,0:T(8,128)(2,1)S(1)} %shard_map.121), channel_id=1, replica_groups=mesh['dp'=8,'expert'=32] {'dp'}, dimensions={0} | all-to-all | bytes 6029312 | tf_op jit(solution)/shard_map/all_to_all | solution.py:421
  130.1 1.8 %shard_map.122 = (bf16[2048,256]{1,0:T(8,128)(2,1)}, bf16[16,256]{1,0:T(8,128)(2,1)S(1)}, bf16[1536,256]{1,0:T(8,128)(2,1)}) custom-call(bf16[8,368,512]{2,1,0:T(8,128)(2,1)S(1)} %all_to_all.22.c_ref, bf16[8,352,512]{2,1,0:T(8,128)(2,1)S(1)} %all_to_all.21.a_ref, bf16[1536,512]{1,0:T(8,128)(2,1)S(1)} %bitcast.23, ...), custom_call_target="tpu_custom_call" | custom-call | tf_op jit(solution)/shard_map/pallas_call | solution.py:46
  131.9 9.5 %all-to-all-start.3 = ((bf16[256,8,256]{2,1,0:T(8,128)(2,1)}), bf16[256,8,256]{2,1,0:T(8,128)(2,1)}, u32[]{:S(2)}, u32[]{:S(2)}) async-start(bf16[256,8,256]{2,1,0:T(8,128)(2,1)} %bitcast.31), calls=%async_computation.3 | async-start | bytes 2097152 | tf_op jit(solution)/shard_map/all_to_all | solution.py:421
  141.4 2.3 %collective-permute-start = (bf16[16,256]{1,0:T(8,128)(2,1)S(1)}, bf16[16,256]{1,0:T(8,128)(2,1)S(1)}, u32[]{:S(2)}, u32[]{:S(2)}) collective-permute-start(bf16[16,256]{1,0:T(8,128)(2,1)S(1)} %get-tuple-element.34), channel_id=1, source_target_pairs={{0,1},{1,0},{2,3},{3,2},{4,5},{5,4},{6,7},{7,6},{8,9},{9,8},{10,11... | collective-permute-start | bytes 24584 | tf_op jit(solution)/shard_map/ppermute | solution.py:388
  143.7 0.8 collective-permute-done
  144.6 0.0 collective-permute-start.1
  144.6 1.9 %collective-permute-start.2 = (bf16[32,256]{1,0:T(8,128)(2,1)S(1)}, bf16[32,256]{1,0:T(8,128)(2,1)S(1)}, u32[]{:S(2)}, u32[]{:S(2)}) collective-permute-start(bf16[32,256]{1,0:T(8,128)(2,1)S(1)} %get-tuple-element.56), channel_id=1, source_target_pairs={{0,16},{1,17},{2,18},{3,19},{4,20},{5,21},{6,22},{7,23},{8,24},{9,... | collective-permute-start | bytes 49160 | tf_op jit(solution)/shard_map/ppermute | solution.py:388
  146.5 1.2 collective-permute-start.3
  147.7 1.1 collective-permute-done.1
  148.8 0.6 collective-permute-done.2
  149.4 0.3 collective-permute-done.3
  149.7 2.3 %collective-permute-start.4 = (bf16[128,256]{1,0:T(8,128)(2,1)S(1)}, bf16[128,256]{1,0:T(8,128)(2,1)S(1)}, u32[]{:S(2)}, u32[]{:S(2)}) collective-permute-start(bf16[128,256]{1,0:T(8,128)(2,1)S(1)} %get-tuple-element.48), channel_id=1, source_target_pairs={{0,2},{1,3},{2,4},{3,5},{4,6},{5,7},{6,0},{7,1},{8,10},{9,11},{10,... | collective-permute-start | bytes 196616 | tf_op jit(solution)/shard_map/ppermute | solution.py:388
  152.1 4.6 %collective-permute-start.5 = (bf16[128,256]{1,0:T(8,128)(2,1)S(1)}, bf16[128,256]{1,0:T(8,128)(2,1)S(1)}, u32[]{:S(2)}, u32[]{:S(2)}) collective-permute-start(bf16[128,256]{1,0:T(8,128)(2,1)S(1)} %get-tuple-element.48), channel_id=1, source_target_pairs={{0,4},{1,5},{2,6},{3,7},{4,0},{5,1},{6,2},{7,3},{8,12},{9,13},{10,... | collective-permute-start | bytes 196616 | tf_op jit(solution)/shard_map/ppermute | solution.py:388
  156.6 2.7 %collective-permute-start.6 = (bf16[128,256]{1,0:T(8,128)(2,1)S(1)}, bf16[128,256]{1,0:T(8,128)(2,1)S(1)}, u32[]{:S(2)}, u32[]{:S(2)}) collective-permute-start(bf16[128,256]{1,0:T(8,128)(2,1)S(1)} %get-tuple-element.48), channel_id=1, source_target_pairs={{0,6},{1,7},{2,0},{3,1},{4,2},{5,3},{6,4},{7,5},{8,14},{9,15},{10,... | collective-permute-start | bytes 196616 | tf_op jit(solution)/shard_map/ppermute | solution.py:388
  159.3 1.1 copy-done.4
  160.4 0.9 copy-done.6
  161.4 3.1 %shard_map.124 = (bf16[192,4096]{1,0:T(8,128)(2,1)}, bf16[192,4096]{1,0:T(8,128)(2,1)}, bf16[1536,512]{1,0:T(8,128)(2,1)}) custom-call(bf16[192,256]{1,0:T(8,128)(2,1)S(1)} %get-tuple-element.42.dh_ref, bf16[192,256]{1,0:T(8,128)(2,1)S(1)} %get-tuple-element.30.du_ref, bf16[1536,256]{1,0:T(8,128)(2,1)S(1)} %copy-done.4, bf16[256,512]{1,0:T(8,128)(2,1)S(1)} %copy-done.6, ...), custom_call_target="tpu_custom_call" | custom-call | tf_op jit(solution)/shard_map/pallas_call | solution.py:46
  164.5 4.3 %collective-permute-done.4 = bf16[128,256]{1,0:T(8,128)(2,1)S(1)} collective-permute-done((bf16[128,256]{1,0:T(8,128)(2,1)S(1)}, bf16[128,256]{1,0:T(8,128)(2,1)S(1)}, u32[]{:S(2)}, u32[]{:S(2)}) %collective-permute-start.4) | collective-permute-done | bytes 65568 | tf_op jit(solution)/shard_map/ppermute | solution.py:388
  168.9 5.1 %collective-permute-done.5 = bf16[128,256]{1,0:T(8,128)(2,1)S(1)} collective-permute-done((bf16[128,256]{1,0:T(8,128)(2,1)S(1)}, bf16[128,256]{1,0:T(8,128)(2,1)S(1)}, u32[]{:S(2)}, u32[]{:S(2)}) %collective-permute-start.5) | collective-permute-done | bytes 65568 | tf_op jit(solution)/shard_map/ppermute | solution.py:388
  174.0 0.0 collective-permute-done.6
  174.0 0.0 all-to-all-done.3
  174.0 4.2 %shard_map.123 = (bf16[64,4096]{1,0:T(8,128)(2,1)}, bf16[64,4096]{1,0:T(8,128)(2,1)}, f32[32,4096]{1,0:T(8,128)}) custom-call(s32[1]{0:T(128)} %bitcast.src_ref, bf16[512,256]{1,0:T(8,128)(2,1)S(1)} %constant_dynamic-update-slice_fusion.7.r_ref, bf16[2048,256]{1,0:T(8,128)(2,1)} %bitcast.11.refs_0_, bf16[64,256]{1,0:T(8,128)(2,1)} %get-tuple-element.36.refs_1_, ...), custom_call_target="tpu_custom_call" | custom-call | tf_op jit(solution)/shard_map/pallas_call | solution.py:46
  (16 shorter events, 0.0 us)
Async XLA Ops:
  0.6 49.5 %copy-start.2 = (bf16[1,1536,512]{2,1,0:T(8,128)(2,1)S(1)}, bf16[1,1536,512]{2,1,0:T(8,128)(2,1)}, u32[]{:S(2)}) copy-start(bf16[1,1536,512]{2,1,0:T(8,128)(2,1)} %param.13) | copy-start | bytes 4718596
  51.9 38.0 %copy-start.5 = (bf16[256,512]{1,0:T(8,128)(2,1)}, bf16[256,512]{1,0:T(8,128)(2,1)S(1)}, u32[]{:S(2)}) copy-start(bf16[256,512]{1,0:T(8,128)(2,1)S(1)} %get-tuple-element.44.gated_ref) | copy-start | bytes 786436
  51.9 37.9 %copy-start = (bf16[1,192,4096]{2,1,0:T(8,128)(2,1)S(1)}, bf16[1,192,4096]{2,1,0:T(8,128)(2,1)}, u32[]{:S(2)}) copy-start(bf16[1,192,4096]{2,1,0:T(8,128)(2,1)} %param.11) | copy-start | bytes 4718596
  51.9 37.9 %copy-start.1 = (bf16[1,192,4096]{2,1,0:T(8,128)(2,1)S(1)}, bf16[1,192,4096]{2,1,0:T(8,128)(2,1)}, u32[]{:S(2)}) copy-start(bf16[1,192,4096]{2,1,0:T(8,128)(2,1)} %param.12) | copy-start | bytes 4718596
  51.9 37.9 %copy-start.3 = (bf16[4096,32]{0,1:T(8,128)(2,1)S(1)}, bf16[4096,32]{0,1:T(8,128)(2,1)}, u32[]{:S(2)}) copy-start(bf16[4096,32]{0,1:T(8,128)(2,1)} %param.9) | copy-start | bytes 786436
  131.9 42.1 %all-to-all-start.3 = ((bf16[256,8,256]{2,1,0:T(8,128)(2,1)}), bf16[256,8,256]{2,1,0:T(8,128)(2,1)}, u32[]{:S(2)}, u32[]{:S(2)}) async-start(bf16[256,8,256]{2,1,0:T(8,128)(2,1)} %bitcast.31), calls=%async_computation.3 | async-start | bytes 2097152 | tf_op jit(solution)/shard_map/all_to_all | solution.py:421
  141.4 3.1 %collective-permute-start = (bf16[16,256]{1,0:T(8,128)(2,1)S(1)}, bf16[16,256]{1,0:T(8,128)(2,1)S(1)}, u32[]{:S(2)}, u32[]{:S(2)}) collective-permute-start(bf16[16,256]{1,0:T(8,128)(2,1)S(1)} %get-tuple-element.34), channel_id=1, source_target_pairs={{0,1},{1,0},{2,3},{3,2},{4,5},{5,4},{6,7},{7,6},{8,9},{9,8},{10,11... | collective-permute-start | bytes 24584 | tf_op jit(solution)/shard_map/ppermute | solution.py:388
  144.6 4.2 %collective-permute-start.1 = (bf16[32,256]{1,0:T(8,128)(2,1)S(1)}, bf16[32,256]{1,0:T(8,128)(2,1)S(1)}, u32[]{:S(2)}, u32[]{:S(2)}) collective-permute-start(bf16[32,256]{1,0:T(8,128)(2,1)S(1)} %get-tuple-element.56), channel_id=1, source_target_pairs={{0,8},{1,9},{2,10},{3,11},{4,12},{5,13},{6,14},{7,15},{8,16},{9,17... | collective-permute-start | bytes 49160 | tf_op jit(solution)/shard_map/ppermute | solution.py:388
  144.6 4.9 %collective-permute-start.2 = (bf16[32,256]{1,0:T(8,128)(2,1)S(1)}, bf16[32,256]{1,0:T(8,128)(2,1)S(1)}, u32[]{:S(2)}, u32[]{:S(2)}) collective-permute-start(bf16[32,256]{1,0:T(8,128)(2,1)S(1)} %get-tuple-element.56), channel_id=1, source_target_pairs={{0,16},{1,17},{2,18},{3,19},{4,20},{5,21},{6,22},{7,23},{8,24},{9,... | collective-permute-start | bytes 49160 | tf_op jit(solution)/shard_map/ppermute | solution.py:388
  146.5 3.2 %collective-permute-start.3 = (bf16[32,256]{1,0:T(8,128)(2,1)S(1)}, bf16[32,256]{1,0:T(8,128)(2,1)S(1)}, u32[]{:S(2)}, u32[]{:S(2)}) collective-permute-start(bf16[32,256]{1,0:T(8,128)(2,1)S(1)} %get-tuple-element.56), channel_id=1, source_target_pairs={{0,24},{1,25},{2,26},{3,27},{4,28},{5,29},{6,30},{7,31},{8,0},{9,1... | collective-permute-start | bytes 49160 | tf_op jit(solution)/shard_map/ppermute | solution.py:388
  149.7 19.1 %collective-permute-start.4 = (bf16[128,256]{1,0:T(8,128)(2,1)S(1)}, bf16[128,256]{1,0:T(8,128)(2,1)S(1)}, u32[]{:S(2)}, u32[]{:S(2)}) collective-permute-start(bf16[128,256]{1,0:T(8,128)(2,1)S(1)} %get-tuple-element.48), channel_id=1, source_target_pairs={{0,2},{1,3},{2,4},{3,5},{4,6},{5,7},{6,0},{7,1},{8,10},{9,11},{10,... | collective-permute-start | bytes 196616 | tf_op jit(solution)/shard_map/ppermute | solution.py:388
  152.1 21.9 %collective-permute-start.5 = (bf16[128,256]{1,0:T(8,128)(2,1)S(1)}, bf16[128,256]{1,0:T(8,128)(2,1)S(1)}, u32[]{:S(2)}, u32[]{:S(2)}) collective-permute-start(bf16[128,256]{1,0:T(8,128)(2,1)S(1)} %get-tuple-element.48), channel_id=1, source_target_pairs={{0,4},{1,5},{2,6},{3,7},{4,0},{5,1},{6,2},{7,3},{8,12},{9,13},{10,... | collective-permute-start | bytes 196616 | tf_op jit(solution)/shard_map/ppermute | solution.py:388
  156.6 17.3 %collective-permute-start.6 = (bf16[128,256]{1,0:T(8,128)(2,1)S(1)}, bf16[128,256]{1,0:T(8,128)(2,1)S(1)}, u32[]{:S(2)}, u32[]{:S(2)}) collective-permute-start(bf16[128,256]{1,0:T(8,128)(2,1)S(1)} %get-tuple-element.48), channel_id=1, source_target_pairs={{0,6},{1,7},{2,0},{3,1},{4,2},{5,3},{6,4},{7,5},{8,14},{9,15},{10,... | collective-permute-start | bytes 196616 | tf_op jit(solution)/shard_map/ppermute | solution.py:388
  159.3 1.1 copy-start.4
  160.4 0.9 copy-start.6

commit v4 on v3

--- a/solution.py
+++ b/solution.py
@@ -33,10 +33,7 @@
 
 def pieces(x):
     hi = x.astype(BF16)
-    rest = x - hi.astype(F32)
-    mid = rest.astype(BF16)
-    low = (rest - mid.astype(F32)).astype(BF16)
-    return hi, mid, low
+    return hi, (x - hi.astype(F32)).astype(BF16)
 
 
 def call(kernel, outs, args, far_in=(), far_out=(), scratch=()):
@@ -251,7 +248,7 @@
         z_ref[at, :] = nn(pick_ref[at, :], y).astype(BF16)
         copies.append(pltpu.make_async_copy(z_ref.at[at], z_out.at[at], sem.at[g]))
         copies[-1].start()
-    dlogit = packed[:1, :rows_n] + packed[1:2, :rows_n] + packed[2:3, :rows_n]
+    dlogit = packed[:1, :rows_n] + packed[1:2, :rows_n]
     terms = [p.astype(F32) for p in pieces(dlogit)]
     terms = jnp.concatenate(terms + [jnp.zeros((8 - len(terms), rows_n), F32)], axis=0).astype(BF16)
     part = r_ref.shape[1]
@@ -349,10 +346,10 @@
     n_rows, part = r_ref.shape
     lines = n_rows // experts
     me = src_ref[0]
-    me_x, me_z, me_c = me // 8, (me // 2) % 4, me % 2
+    me_x, me_z = me // 8, (me // 2) % 4
     row, col = iota((n_rows, n_rows), 0), iota((n_rows, n_rows), 1)
     block = col // lines
-    source = ((me_x + 4 - (block // 2) % 4) % 4) * 8 + ((me_z + 4 - block // 8) % 4) * 2 + (me_c + block) % 2
+    source = ((me_x + 4 - (block // 2) % 4) % 4) * 8 + ((me_z + 4 - block // 8) % 4) * 2 + block % 2
     sort = ((row % experts == source) & (row // experts == col % lines)).astype(BF16)
     rgrad = nn(sort, r_ref[...])
     for i in range(lines):
@@ -369,7 +366,7 @@
     for d in range(0, n_dp, 2):
         diffs = nn(pick, both(d, slice(LANES, 2 * LANES)))
         router = router_ref[:, d * cols : (d + 2) * cols]
-        from_router = nn(terms, jnp.concatenate([router] * 3, axis=0))
+        from_router = nn(terms, jnp.concatenate([router] * 2, axis=0))
         for i in range(2):
             for c in range(chunks):
                 at = i * cols + c * LANES
@@ -383,23 +380,28 @@
     wait(tgrad_back)
 
 
+def shifted(x, k, to):
+    return lax.ppermute(x, "expert", [(e, to(e, k)) for e in range(32)])
+
+
+def paired(x, axis):
+    got = shifted(x, 1, lambda e, k: e ^ k)
+    first = lax.axis_index("expert") % 2 == 0
+    return jnp.where(first, jnp.concatenate([x, got], axis), jnp.concatenate([got, x], axis))
+
+
 def spread(r):
-    def shifted(x, k, to):
-        return lax.ppermute(x, "expert", [(e, to(e, k)) for e in range(32)])
-
-    def core(e, k):
-        return e // 2 * 2 + (e + k) % 2
-
     def along_x(e, k):
         return (e + 8 * k) % 32
 
     def along_z(e, k):
         return e // 8 * 8 + (e + 2 * k) % 8
 
-    for to, n in ((core, 2), (along_x, 4), (along_z, 4)):
-        half = r
-        r = jnp.concatenate([r] + [shifted(r, k, to) for k in range(1, n)], axis=0)
-    return r, half
+    r = paired(r, 0)
+    r = jnp.concatenate([r] + [shifted(r, k, along_x) for k in range(1, 4)], axis=0)
+    middle = r.shape[1] // 2
+    half = jnp.where(lax.axis_index("expert") % 2 == 0, r[:, :middle], r[:, middle:])
+    return jnp.concatenate([half] + [shifted(half, k, along_z) for k in range(1, 4)], axis=0)
 
 
 def local(tokens, out_grad, router, choice_index, gate_weight, up_weight, down_weight):
@@ -467,14 +469,15 @@
         ],
     )
     z = swap(z.reshape(n_dp * experts, per, 2 * LANES), ("dp", "expert"))
-    r, half = spread(r)
-    dh, half = lax.optimization_barrier((dh, half))
+    r = spread(r)
     gate_grad, up_grad, down_grad = call(
         weight_kernel,
         [((units, width), BF16), ((units, width), BF16), ((n_dp * units, cols), BF16)],
         (dh, du, act, gated, a),
     )
     taken = (z.reshape(n_dp * slots, 2 * LANES), sel, gsel, gates, grad, router)
+    r, gate_grad, up_grad, down_grad = lax.optimization_barrier((r, gate_grad, up_grad, down_grad))
+    r = paired(r, 1)
     results = [((tok_count, width), BF16), ((tok_count, width), BF16), ((experts, width), F32)]
     mixed, token_grad, router_grad = call(
         take_kernel,

time: 179 us -> 178 us (level)
    ppermute x7 -> x8, waiting for transfers between devices: 12.3 us -> 11.5 us  [shifted(): return lax.ppermute(x, 'expert', [(e, to(e, k)) for e in range(32)])]
    ppermute x7 -> x8, starting transfers between devices: 15 us -> 15.7 us  [shifted(): return lax.ppermute(x, 'expert', [(e, to(e, k)) for e in range(32)])]
  transfers between devices with their start and end apart: 8 -> 9, of which waited for: 6 -> 7; matrix products, arithmetic and copies ran while one was open for 0% -> 0% of each run, Pallas kernels for 2% -> 2%
where the time goes in v4:
time: 178 us; the launch traced here: 177 us
  blocking collectives  122 us (69%)
  starting transfers between devices  25.2 us (14%)
  Pallas kernels  16.2 us (9%)
  waiting for transfers between devices  11.5 us (6%)
    all_to_all x3, blocking collectives, swap(): return lax.all_to_all(x, axis, split_axis=0, concat_axis=0, tiled=True)  122 us
    pallas_call x7, Pallas kernels, call(): pl.pallas_call(kernel, out_shape=tuple((pltpu.HBM(s, d) if i in far_out e...  16.2 us
    ppermute x8, starting transfers between devices, shifted(): return lax.ppermute(x, 'expert', [(e, to(e, k)) for e in range(32)])  15.7 us
    ppermute x8, waiting for transfers between devices, shifted(): return lax.ppermute(x, 'expert', [(e, to(e, k)) for e in range(32)])  11.5 us
    all_to_all x1, starting transfers between devices, swap(): return lax.all_to_all(x, axis, split_axis=0, concat_axis=0, tiled=True)  9.54 us
  transfers between devices with their start and end apart: 9, of which 7 were waited for; matrix products, arithmetic and copies ran while one was open for 0% of the time, Pallas kernels for 2%

profile of v4, /device:TPU:1, one launch (start us, length us, event | category | flops | bytes accessed | tf_op | source)
XLA Modules:
  0.0 177.4 jit_solution(13320300803624034669)
XLA Ops:
  0.6 2.8 %shard_map.118 = (bf16[8,256,256]{2,1,0:T(8,128)(2,1)S(1)}, bf16[64,256]{1,0:T(8,128)(2,1)}, f32[64,256]{1,0:T(8,128)}, f32[64,32]{1,0:T(8,128)}) custom-call(s32[1]{0:T(128)} %bitcast.src_ref, s32[32,32]{1,0:T(8,128)} %bitcast.33, bf16[64,4096]{1,0:T(8,128)(2,1)} %bitcast.32, bf16[64,4096]{1,0:T(8,128)(2,1)} %bitcast.29, bf16[32,4096]{1,0:T(8,128)(2,1)} %bitcast.25), custom_call_target="tpu_custom_call" | custom-call | tf_op jit(solution)/shard_map/pallas_call | solution.py:43
  3.5 46.6 %all_to_all.20 = bf16[256,8,256]{2,1,0:T(8,128)(2,1)S(1)} all-to-all(bf16[256,8,256]{2,1,0:T(8,128)(2,1)S(1)} %bitcast.28), channel_id=1, replica_groups=mesh['dp'=8,'expert'=32] {'dp','expert'}, dimensions={0} | all-to-all | bytes 2097152 | tf_op jit(solution)/shard_map/all_to_all | solution.py:423
  50.1 1.7 shard_map.119
  51.8 0.0 copy-start.5
  51.9 0.0 copy-start
  51.9 0.0 copy-start.1
  51.9 0.0 copy-start.3
  51.9 37.9 %all_to_all.21.a_ref = bf16[8,352,512]{2,1,0:T(8,128)(2,1)S(1)} all-to-all(bf16[8,352,512]{2,1,0:T(8,128)(2,1)S(1)} %get-tuple-element.31), channel_id=1, replica_groups=mesh['dp'=8,'expert'=32] {'dp'}, dimensions={0} | all-to-all | bytes 5767168 | tf_op jit(solution)/shard_map/all_to_all | solution.py:423
  89.8 1.2 shard_map.120
  91.0 1.3 shard_map.121
  92.3 37.7 %all_to_all.22.c_ref = bf16[8,368,512]{2,1,0:T(8,128)(2,1)S(1)} all-to-all(bf16[8,368,512]{2,1,0:T(8,128)(2,1)S(1)} %shard_map.121), channel_id=1, replica_groups=mesh['dp'=8,'expert'=32] {'dp'}, dimensions={0} | all-to-all | bytes 6029312 | tf_op jit(solution)/shard_map/all_to_all | solution.py:423
  130.0 1.8 %shard_map.122 = (bf16[2048,256]{1,0:T(8,128)(2,1)}, bf16[16,256]{1,0:T(8,128)(2,1)S(1)}, bf16[1536,256]{1,0:T(8,128)(2,1)}) custom-call(bf16[8,368,512]{2,1,0:T(8,128)(2,1)S(1)} %all_to_all.22.c_ref, bf16[8,352,512]{2,1,0:T(8,128)(2,1)S(1)} %all_to_all.21.a_ref, bf16[1536,512]{1,0:T(8,128)(2,1)S(1)} %bitcast.23, ...), custom_call_target="tpu_custom_call" | custom-call | tf_op jit(solution)/shard_map/pallas_call | solution.py:43
  131.8 0.0 copy-start.6
  131.8 9.5 %all-to-all-start.3 = ((bf16[256,8,256]{2,1,0:T(8,128)(2,1)}), bf16[256,8,256]{2,1,0:T(8,128)(2,1)}, u32[]{:S(2)}, u32[]{:S(2)}) async-start(bf16[256,8,256]{2,1,0:T(8,128)(2,1)} %bitcast.31), calls=%async_computation.3 | async-start | bytes 2097152 | tf_op jit(solution)/shard_map/all_to_all | solution.py:423
  141.4 2.4 %collective-permute-start = (bf16[16,256]{1,0:T(8,128)(2,1)S(1)}, bf16[16,256]{1,0:T(8,128)(2,1)S(1)}, u32[]{:S(2)}, u32[]{:S(2)}) collective-permute-start(bf16[16,256]{1,0:T(8,128)(2,1)S(1)} %get-tuple-element.37), channel_id=1, source_target_pairs={{0,1},{1,0},{2,3},{3,2},{4,5},{5,4},{6,7},{7,6},{8,9},{9,8},{10,11... | collective-permute-start | bytes 24584 | tf_op jit(solution)/shard_map/ppermute | solution.py:384
  143.8 0.8 collective-permute-done
  144.7 1.8 %collective-permute-start.2 = (bf16[32,256]{1,0:T(8,128)(2,1)S(1)}, bf16[32,256]{1,0:T(8,128)(2,1)S(1)}, u32[]{:S(2)}, u32[]{:S(2)}) collective-permute-start(bf16[32,256]{1,0:T(8,128)(2,1)S(1)} %maximum_select_fusion.1), channel_id=1, source_target_pairs={{0,16},{1,17},{2,18},{3,19},{4,20},{5,21},{6,22},{7,23},{8,24},{9,... | collective-permute-start | bytes 49160 | tf_op jit(solution)/shard_map/ppermute | solution.py:384
  146.5 1.2 collective-permute-start.3
  147.7 1.3 collective-permute-done.1
  148.9 0.6 collective-permute-done.2
  149.5 0.3 collective-permute-done.3
  149.8 2.4 %collective-permute-start.4 = (bf16[128,128]{1,0:T(8,128)(2,1)S(1)}, bf16[128,128]{1,0:T(8,128)(2,1)S(1)}, u32[]{:S(2)}, u32[]{:S(2)}) collective-permute-start(bf16[128,128]{1,0:T(8,128)(2,1)S(1)} %slice_select_fusion), channel_id=1, source_target_pairs={{0,2},{1,3},{2,4},{3,5},{4,6},{5,7},{6,0},{7,1},{8,10},{9,11},{10,... | collective-permute-start | bytes 98312 | tf_op jit(solution)/shard_map/ppermute | solution.py:384
  152.2 4.5 %collective-permute-start.5 = (bf16[128,128]{1,0:T(8,128)(2,1)S(1)}, bf16[128,128]{1,0:T(8,128)(2,1)S(1)}, u32[]{:S(2)}, u32[]{:S(2)}) collective-permute-start(bf16[128,128]{1,0:T(8,128)(2,1)S(1)} %slice_select_fusion), channel_id=1, source_target_pairs={{0,4},{1,5},{2,6},{3,7},{4,0},{5,1},{6,2},{7,3},{8,12},{9,13},{10,... | collective-permute-start | bytes 98312 | tf_op jit(solution)/shard_map/ppermute | solution.py:384
  156.7 2.7 %collective-permute-start.6 = (bf16[128,128]{1,0:T(8,128)(2,1)S(1)}, bf16[128,128]{1,0:T(8,128)(2,1)S(1)}, u32[]{:S(2)}, u32[]{:S(2)}) collective-permute-start(bf16[128,128]{1,0:T(8,128)(2,1)S(1)} %slice_select_fusion), channel_id=1, source_target_pairs={{0,6},{1,7},{2,0},{3,1},{4,2},{5,3},{6,4},{7,5},{8,14},{9,15},{10,... | collective-permute-start | bytes 98312 | tf_op jit(solution)/shard_map/ppermute | solution.py:384
  159.5 1.1 copy-done.4
  160.6 3.1 %shard_map.123 = (bf16[192,4096]{1,0:T(8,128)(2,1)}, bf16[192,4096]{1,0:T(8,128)(2,1)}, bf16[1536,512]{1,0:T(8,128)(2,1)}) custom-call(bf16[192,256]{1,0:T(8,128)(2,1)S(1)} %get-tuple-element.32.dh_ref, bf16[192,256]{1,0:T(8,128)(2,1)S(1)} %get-tuple-element.33.du_ref, bf16[1536,256]{1,0:T(8,128)(2,1)S(1)} %copy-done.4, bf16[256,512]{1,0:T(8,128)(2,1)S(1)} %copy-done.6, ...), custom_call_target="tpu_custom_call" | custom-call | tf_op jit(solution)/shard_map/pallas_call | solution.py:43
  163.7 4.0 %collective-permute-done.4 = bf16[128,128]{1,0:T(8,128)(2,1)S(1)} collective-permute-done((bf16[128,128]{1,0:T(8,128)(2,1)S(1)}, bf16[128,128]{1,0:T(8,128)(2,1)S(1)}, u32[]{:S(2)}, u32[]{:S(2)}) %collective-permute-start.4) | collective-permute-done | bytes 32800 | tf_op jit(solution)/shard_map/ppermute | solution.py:384
  167.8 3.5 %collective-permute-done.5 = bf16[128,128]{1,0:T(8,128)(2,1)S(1)} collective-permute-done((bf16[128,128]{1,0:T(8,128)(2,1)S(1)}, bf16[128,128]{1,0:T(8,128)(2,1)S(1)}, u32[]{:S(2)}, u32[]{:S(2)}) %collective-permute-start.5) | collective-permute-done | bytes 32800 | tf_op jit(solution)/shard_map/ppermute | solution.py:384
  171.3 0.6 collective-permute-start.7
  171.9 1.0 collective-permute-done.7
  172.9 0.1 maximum_select_fusion.r_ref
  173.0 4.3 %shard_map.124 = (bf16[64,4096]{1,0:T(8,128)(2,1)}, bf16[64,4096]{1,0:T(8,128)(2,1)}, f32[32,4096]{1,0:T(8,128)}) custom-call(s32[1]{0:T(128)} %bitcast.src_ref, bf16[512,256]{1,0:T(8,128)(2,1)S(1)} %maximum_select_fusion.r_ref, bf16[2048,256]{1,0:T(8,128)(2,1)} %bitcast.11.refs_0_, bf16[64,256]{1,0:T(8,128)(2,1)} %get-tuple-element.45.refs_1_, ...), custom_call_target="tpu_custom_call" | custom-call | tf_op jit(solution)/shard_map/pallas_call | solution.py:43
  (15 shorter events, 0.1 us)
Async XLA Ops:
  0.6 49.5 %copy-start.2 = (bf16[1,1536,512]{2,1,0:T(8,128)(2,1)S(1)}, bf16[1,1536,512]{2,1,0:T(8,128)(2,1)}, u32[]{:S(2)}) copy-start(bf16[1,1536,512]{2,1,0:T(8,128)(2,1)} %param.13) | copy-start | bytes 4718596
  51.8 38.0 %copy-start.5 = (bf16[256,512]{1,0:T(8,128)(2,1)}, bf16[256,512]{1,0:T(8,128)(2,1)S(1)}, u32[]{:S(2)}) copy-start(bf16[256,512]{1,0:T(8,128)(2,1)S(1)} %get-tuple-element.39.gated_ref) | copy-start | bytes 786436
  51.9 38.0 %copy-start = (bf16[1,192,4096]{2,1,0:T(8,128)(2,1)S(1)}, bf16[1,192,4096]{2,1,0:T(8,128)(2,1)}, u32[]{:S(2)}) copy-start(bf16[1,192,4096]{2,1,0:T(8,128)(2,1)} %param.11) | copy-start | bytes 4718596
  51.9 37.9 %copy-start.1 = (bf16[1,192,4096]{2,1,0:T(8,128)(2,1)S(1)}, bf16[1,192,4096]{2,1,0:T(8,128)(2,1)}, u32[]{:S(2)}) copy-start(bf16[1,192,4096]{2,1,0:T(8,128)(2,1)} %param.12) | copy-start | bytes 4718596
  51.9 37.9 %copy-start.3 = (bf16[4096,32]{0,1:T(8,128)(2,1)S(1)}, bf16[4096,32]{0,1:T(8,128)(2,1)}, u32[]{:S(2)}) copy-start(bf16[4096,32]{0,1:T(8,128)(2,1)} %param.9) | copy-start | bytes 786436
  131.8 27.7 %copy-start.6 = (bf16[256,512]{1,0:T(8,128)(2,1)S(1)}, bf16[256,512]{1,0:T(8,128)(2,1)}, u32[]{:S(2)}) copy-start(bf16[256,512]{1,0:T(8,128)(2,1)} %copy-done.5) | copy-start | bytes 786436
  131.8 41.1 %all-to-all-start.3 = ((bf16[256,8,256]{2,1,0:T(8,128)(2,1)}), bf16[256,8,256]{2,1,0:T(8,128)(2,1)}, u32[]{:S(2)}, u32[]{:S(2)}) async-start(bf16[256,8,256]{2,1,0:T(8,128)(2,1)} %bitcast.31), calls=%async_computation.3 | async-start | bytes 2097152 | tf_op jit(solution)/shard_map/all_to_all | solution.py:423
  141.4 3.3 %collective-permute-start = (bf16[16,256]{1,0:T(8,128)(2,1)S(1)}, bf16[16,256]{1,0:T(8,128)(2,1)S(1)}, u32[]{:S(2)}, u32[]{:S(2)}) collective-permute-start(bf16[16,256]{1,0:T(8,128)(2,1)S(1)} %get-tuple-element.37), channel_id=1, source_target_pairs={{0,1},{1,0},{2,3},{3,2},{4,5},{5,4},{6,7},{7,6},{8,9},{9,8},{10,11... | collective-permute-start | bytes 24584 | tf_op jit(solution)/shard_map/ppermute | solution.py:384
  144.7 4.2 %collective-permute-start.1 = (bf16[32,256]{1,0:T(8,128)(2,1)S(1)}, bf16[32,256]{1,0:T(8,128)(2,1)S(1)}, u32[]{:S(2)}, u32[]{:S(2)}) collective-permute-start(bf16[32,256]{1,0:T(8,128)(2,1)S(1)} %maximum_select_fusion.1), channel_id=1, source_target_pairs={{0,8},{1,9},{2,10},{3,11},{4,12},{5,13},{6,14},{7,15},{8,16},{9,17... | collective-permute-start | bytes 49160 | tf_op jit(solution)/shard_map/ppermute | solution.py:384
  144.7 4.8 %collective-permute-start.2 = (bf16[32,256]{1,0:T(8,128)(2,1)S(1)}, bf16[32,256]{1,0:T(8,128)(2,1)S(1)}, u32[]{:S(2)}, u32[]{:S(2)}) collective-permute-start(bf16[32,256]{1,0:T(8,128)(2,1)S(1)} %maximum_select_fusion.1), channel_id=1, source_target_pairs={{0,16},{1,17},{2,18},{3,19},{4,20},{5,21},{6,22},{7,23},{8,24},{9,... | collective-permute-start | bytes 49160 | tf_op jit(solution)/shard_map/ppermute | solution.py:384
  146.5 3.3 %collective-permute-start.3 = (bf16[32,256]{1,0:T(8,128)(2,1)S(1)}, bf16[32,256]{1,0:T(8,128)(2,1)S(1)}, u32[]{:S(2)}, u32[]{:S(2)}) collective-permute-start(bf16[32,256]{1,0:T(8,128)(2,1)S(1)} %maximum_select_fusion.1), channel_id=1, source_target_pairs={{0,24},{1,25},{2,26},{3,27},{4,28},{5,29},{6,30},{7,31},{8,0},{9,1... | collective-permute-start | bytes 49160 | tf_op jit(solution)/shard_map/ppermute | solution.py:384
  149.8 17.9 %collective-permute-start.4 = (bf16[128,128]{1,0:T(8,128)(2,1)S(1)}, bf16[128,128]{1,0:T(8,128)(2,1)S(1)}, u32[]{:S(2)}, u32[]{:S(2)}) collective-permute-start(bf16[128,128]{1,0:T(8,128)(2,1)S(1)} %slice_select_fusion), channel_id=1, source_target_pairs={{0,2},{1,3},{2,4},{3,5},{4,6},{5,7},{6,0},{7,1},{8,10},{9,11},{10,... | collective-permute-start | bytes 98312 | tf_op jit(solution)/shard_map/ppermute | solution.py:384
  152.2 19.0 %collective-permute-start.5 = (bf16[128,128]{1,0:T(8,128)(2,1)S(1)}, bf16[128,128]{1,0:T(8,128)(2,1)S(1)}, u32[]{:S(2)}, u32[]{:S(2)}) collective-permute-start(bf16[128,128]{1,0:T(8,128)(2,1)S(1)} %slice_select_fusion), channel_id=1, source_target_pairs={{0,4},{1,5},{2,6},{3,7},{4,0},{5,1},{6,2},{7,3},{8,12},{9,13},{10,... | collective-permute-start | bytes 98312 | tf_op jit(solution)/shard_map/ppermute | solution.py:384
  156.7 14.5 %collective-permute-start.6 = (bf16[128,128]{1,0:T(8,128)(2,1)S(1)}, bf16[128,128]{1,0:T(8,128)(2,1)S(1)}, u32[]{:S(2)}, u32[]{:S(2)}) collective-permute-start(bf16[128,128]{1,0:T(8,128)(2,1)S(1)} %slice_select_fusion), channel_id=1, source_target_pairs={{0,6},{1,7},{2,0},{3,1},{4,2},{5,3},{6,4},{7,5},{8,14},{9,15},{10,... | collective-permute-start | bytes 98312 | tf_op jit(solution)/shard_map/ppermute | solution.py:384
  159.5 1.1 copy-start.4
  171.3 1.6 collective-permute-start.7

commit v5 on v4

--- a/solution.py
+++ b/solution.py
@@ -323,6 +323,7 @@
     pick = by_chunk(sel_ref[...])
     weights = [by_chunk(w) for w in pieces(gsel_ref[...])]
     hits = jnp.zeros(pick.shape, F32)
+    diffs = []
     for d in range(0, n_dp, 2):
         wait(copies[0][d // 2 : d // 2 + 1])
         outs = both(d, slice(0, LANES))
@@ -343,6 +344,7 @@
             axis=0,
         )
         hits += nt(grads, outs)
+        diffs.append(nn(pick, both(d, slice(LANES, 2 * LANES))))
     n_rows, part = r_ref.shape
     lines = n_rows // experts
     me = src_ref[0]
@@ -364,14 +366,13 @@
     dlogit = sum(nn(p, collect) for p in pieces(hits)) * gates * (1.0 - gates)
     terms = jnp.concatenate(pieces(dlogit), axis=1)
     for d in range(0, n_dp, 2):
-        diffs = nn(pick, both(d, slice(LANES, 2 * LANES)))
         router = router_ref[:, d * cols : (d + 2) * cols]
         from_router = nn(terms, jnp.concatenate([router] * 2, axis=0))
         for i in range(2):
             for c in range(chunks):
                 at = i * cols + c * LANES
                 tgrad_ref[:, span(d + i, c)] = (
-                    diffs[c * tok_count : (c + 1) * tok_count, i * LANES : (i + 1) * LANES]
+                    diffs[d // 2][c * tok_count : (c + 1) * tok_count, i * LANES : (i + 1) * LANES]
                     + from_router[:, at : at + LANES]
                 ).astype(BF16)
         tgrad_back[d // 2].start()

time: 178 us -> 178 us (level)
  no operation moved by 1% of the time
where the time goes in v5:
time: 178 us
  blocking collectives  122 us (69%)
  starting transfers between devices  25.2 us (14%)
  Pallas kernels  16.4 us (9%)
  waiting for transfers between devices  11.5 us (6%)
    all_to_all x3, blocking collectives, swap(): return lax.all_to_all(x, axis, split_axis=0, concat_axis=0, tiled=True)  122 us
    pallas_call x7, Pallas kernels, call(): pl.pallas_call(kernel, out_shape=tuple((pltpu.HBM(s, d) if i in far_out e...  16.4 us
    ppermute x8, starting transfers between devices, shifted(): return lax.ppermute(x, 'expert', [(e, to(e, k)) for e in range(32)])  15.7 us
    ppermute x8, waiting for transfers between devices, shifted(): return lax.ppermute(x, 'expert', [(e, to(e, k)) for e in range(32)])  11.5 us
    all_to_all x1, starting transfers between devices, swap(): return lax.all_to_all(x, axis, split_axis=0, concat_axis=0, tiled=True)  9.54 us
  transfers between devices with their start and end apart: 9, of which 7 were waited for; matrix products, arithmetic and copies ran while one was open for 0% of the time, Pallas kernels for 2%

profile of v5, /device:TPU:1, one launch (start us, length us, event | category | flops | bytes accessed | tf_op | source)
XLA Modules:
  0.0 177.6 jit_solution(4043605603840412583)
XLA Ops:
  0.6 2.8 %shard_map.118 = (bf16[8,256,256]{2,1,0:T(8,128)(2,1)S(1)}, bf16[64,256]{1,0:T(8,128)(2,1)}, f32[64,256]{1,0:T(8,128)}, f32[64,32]{1,0:T(8,128)}) custom-call(s32[1]{0:T(128)} %bitcast.src_ref, s32[32,32]{1,0:T(8,128)} %bitcast.33, bf16[64,4096]{1,0:T(8,128)(2,1)} %bitcast.32, bf16[64,4096]{1,0:T(8,128)(2,1)} %bitcast.29, bf16[32,4096]{1,0:T(8,128)(2,1)} %bitcast.25), custom_call_target="tpu_custom_call" | custom-call | tf_op jit(solution)/shard_map/pallas_call | solution.py:43
  3.5 46.6 %all_to_all.20 = bf16[256,8,256]{2,1,0:T(8,128)(2,1)S(1)} all-to-all(bf16[256,8,256]{2,1,0:T(8,128)(2,1)S(1)} %bitcast.28), channel_id=1, replica_groups=mesh['dp'=8,'expert'=32] {'dp','expert'}, dimensions={0} | all-to-all | bytes 2097152 | tf_op jit(solution)/shard_map/all_to_all | solution.py:424
  50.1 1.7 shard_map.119
  51.8 0.0 copy-start.5
  51.9 0.0 copy-start
  51.9 0.0 copy-start.1
  51.9 0.0 copy-start.3
  51.9 37.9 %all_to_all.21.a_ref = bf16[8,352,512]{2,1,0:T(8,128)(2,1)S(1)} all-to-all(bf16[8,352,512]{2,1,0:T(8,128)(2,1)S(1)} %get-tuple-element.31), channel_id=1, replica_groups=mesh['dp'=8,'expert'=32] {'dp'}, dimensions={0} | all-to-all | bytes 5767168 | tf_op jit(solution)/shard_map/all_to_all | solution.py:424
  89.8 1.2 shard_map.120
  91.0 1.3 shard_map.121
  92.3 37.7 %all_to_all.22.c_ref = bf16[8,368,512]{2,1,0:T(8,128)(2,1)S(1)} all-to-all(bf16[8,368,512]{2,1,0:T(8,128)(2,1)S(1)} %shard_map.121), channel_id=1, replica_groups=mesh['dp'=8,'expert'=32] {'dp'}, dimensions={0} | all-to-all | bytes 6029312 | tf_op jit(solution)/shard_map/all_to_all | solution.py:424
  130.0 1.8 %shard_map.122 = (bf16[2048,256]{1,0:T(8,128)(2,1)}, bf16[16,256]{1,0:T(8,128)(2,1)S(1)}, bf16[1536,256]{1,0:T(8,128)(2,1)}) custom-call(bf16[8,368,512]{2,1,0:T(8,128)(2,1)S(1)} %all_to_all.22.c_ref, bf16[8,352,512]{2,1,0:T(8,128)(2,1)S(1)} %all_to_all.21.a_ref, bf16[1536,512]{1,0:T(8,128)(2,1)S(1)} %bitcast.23, ...), custom_call_target="tpu_custom_call" | custom-call | tf_op jit(solution)/shard_map/pallas_call | solution.py:43
  131.8 0.0 copy-start.6
  131.8 9.5 %all-to-all-start.3 = ((bf16[256,8,256]{2,1,0:T(8,128)(2,1)}), bf16[256,8,256]{2,1,0:T(8,128)(2,1)}, u32[]{:S(2)}, u32[]{:S(2)}) async-start(bf16[256,8,256]{2,1,0:T(8,128)(2,1)} %bitcast.31), calls=%async_computation.3 | async-start | bytes 2097152 | tf_op jit(solution)/shard_map/all_to_all | solution.py:424
  141.4 2.4 %collective-permute-start = (bf16[16,256]{1,0:T(8,128)(2,1)S(1)}, bf16[16,256]{1,0:T(8,128)(2,1)S(1)}, u32[]{:S(2)}, u32[]{:S(2)}) collective-permute-start(bf16[16,256]{1,0:T(8,128)(2,1)S(1)} %get-tuple-element.37), channel_id=1, source_target_pairs={{0,1},{1,0},{2,3},{3,2},{4,5},{5,4},{6,7},{7,6},{8,9},{9,8},{10,11... | collective-permute-start | bytes 24584 | tf_op jit(solution)/shard_map/ppermute | solution.py:385
  143.8 0.8 collective-permute-done
  144.7 1.8 %collective-permute-start.2 = (bf16[32,256]{1,0:T(8,128)(2,1)S(1)}, bf16[32,256]{1,0:T(8,128)(2,1)S(1)}, u32[]{:S(2)}, u32[]{:S(2)}) collective-permute-start(bf16[32,256]{1,0:T(8,128)(2,1)S(1)} %maximum_select_fusion.1), channel_id=1, source_target_pairs={{0,16},{1,17},{2,18},{3,19},{4,20},{5,21},{6,22},{7,23},{8,24},{9,... | collective-permute-start | bytes 49160 | tf_op jit(solution)/shard_map/ppermute | solution.py:385
  146.5 1.2 collective-permute-start.3
  147.7 1.3 collective-permute-done.1
  148.9 0.6 collective-permute-done.2
  149.5 0.3 collective-permute-done.3
  149.8 2.4 %collective-permute-start.4 = (bf16[128,128]{1,0:T(8,128)(2,1)S(1)}, bf16[128,128]{1,0:T(8,128)(2,1)S(1)}, u32[]{:S(2)}, u32[]{:S(2)}) collective-permute-start(bf16[128,128]{1,0:T(8,128)(2,1)S(1)} %slice_select_fusion), channel_id=1, source_target_pairs={{0,2},{1,3},{2,4},{3,5},{4,6},{5,7},{6,0},{7,1},{8,10},{9,11},{10,... | collective-permute-start | bytes 98312 | tf_op jit(solution)/shard_map/ppermute | solution.py:385
  152.2 4.5 %collective-permute-start.5 = (bf16[128,128]{1,0:T(8,128)(2,1)S(1)}, bf16[128,128]{1,0:T(8,128)(2,1)S(1)}, u32[]{:S(2)}, u32[]{:S(2)}) collective-permute-start(bf16[128,128]{1,0:T(8,128)(2,1)S(1)} %slice_select_fusion), channel_id=1, source_target_pairs={{0,4},{1,5},{2,6},{3,7},{4,0},{5,1},{6,2},{7,3},{8,12},{9,13},{10,... | collective-permute-start | bytes 98312 | tf_op jit(solution)/shard_map/ppermute | solution.py:385
  156.7 2.7 %collective-permute-start.6 = (bf16[128,128]{1,0:T(8,128)(2,1)S(1)}, bf16[128,128]{1,0:T(8,128)(2,1)S(1)}, u32[]{:S(2)}, u32[]{:S(2)}) collective-permute-start(bf16[128,128]{1,0:T(8,128)(2,1)S(1)} %slice_select_fusion), channel_id=1, source_target_pairs={{0,6},{1,7},{2,0},{3,1},{4,2},{5,3},{6,4},{7,5},{8,14},{9,15},{10,... | collective-permute-start | bytes 98312 | tf_op jit(solution)/shard_map/ppermute | solution.py:385
  159.5 1.1 copy-done.4
  160.6 3.1 %shard_map.123 = (bf16[192,4096]{1,0:T(8,128)(2,1)}, bf16[192,4096]{1,0:T(8,128)(2,1)}, bf16[1536,512]{1,0:T(8,128)(2,1)}) custom-call(bf16[192,256]{1,0:T(8,128)(2,1)S(1)} %get-tuple-element.32.dh_ref, bf16[192,256]{1,0:T(8,128)(2,1)S(1)} %get-tuple-element.33.du_ref, bf16[1536,256]{1,0:T(8,128)(2,1)S(1)} %copy-done.4, bf16[256,512]{1,0:T(8,128)(2,1)S(1)} %copy-done.6, ...), custom_call_target="tpu_custom_call" | custom-call | tf_op jit(solution)/shard_map/pallas_call | solution.py:43
  163.7 4.0 %collective-permute-done.4 = bf16[128,128]{1,0:T(8,128)(2,1)S(1)} collective-permute-done((bf16[128,128]{1,0:T(8,128)(2,1)S(1)}, bf16[128,128]{1,0:T(8,128)(2,1)S(1)}, u32[]{:S(2)}, u32[]{:S(2)}) %collective-permute-start.4) | collective-permute-done | bytes 32800 | tf_op jit(solution)/shard_map/ppermute | solution.py:385
  167.8 3.5 %collective-permute-done.5 = bf16[128,128]{1,0:T(8,128)(2,1)S(1)} collective-permute-done((bf16[128,128]{1,0:T(8,128)(2,1)S(1)}, bf16[128,128]{1,0:T(8,128)(2,1)S(1)}, u32[]{:S(2)}, u32[]{:S(2)}) %collective-permute-start.5) | collective-permute-done | bytes 32800 | tf_op jit(solution)/shard_map/ppermute | solution.py:385
  171.3 0.6 collective-permute-start.7
  171.9 1.0 collective-permute-done.7
  172.9 0.1 maximum_select_fusion.r_ref
  173.0 4.5 %shard_map.124 = (bf16[64,4096]{1,0:T(8,128)(2,1)}, bf16[64,4096]{1,0:T(8,128)(2,1)}, f32[32,4096]{1,0:T(8,128)}) custom-call(s32[1]{0:T(128)} %bitcast.src_ref, bf16[512,256]{1,0:T(8,128)(2,1)S(1)} %maximum_select_fusion.r_ref, bf16[2048,256]{1,0:T(8,128)(2,1)} %bitcast.11.refs_0_, bf16[64,256]{1,0:T(8,128)(2,1)} %get-tuple-element.45.refs_1_, ...), custom_call_target="tpu_custom_call" | custom-call | tf_op jit(solution)/shard_map/pallas_call | solution.py:43
  (15 shorter events, 0.1 us)
Async XLA Ops:
  0.6 49.5 %copy-start.2 = (bf16[1,1536,512]{2,1,0:T(8,128)(2,1)S(1)}, bf16[1,1536,512]{2,1,0:T(8,128)(2,1)}, u32[]{:S(2)}) copy-start(bf16[1,1536,512]{2,1,0:T(8,128)(2,1)} %param.13) | copy-start | bytes 4718596
  51.8 38.0 %copy-start.5 = (bf16[256,512]{1,0:T(8,128)(2,1)}, bf16[256,512]{1,0:T(8,128)(2,1)S(1)}, u32[]{:S(2)}) copy-start(bf16[256,512]{1,0:T(8,128)(2,1)S(1)} %get-tuple-element.39.gated_ref) | copy-start | bytes 786436
  51.9 38.0 %copy-start = (bf16[1,192,4096]{2,1,0:T(8,128)(2,1)S(1)}, bf16[1,192,4096]{2,1,0:T(8,128)(2,1)}, u32[]{:S(2)}) copy-start(bf16[1,192,4096]{2,1,0:T(8,128)(2,1)} %param.11) | copy-start | bytes 4718596
  51.9 37.9 %copy-start.1 = (bf16[1,192,4096]{2,1,0:T(8,128)(2,1)S(1)}, bf16[1,192,4096]{2,1,0:T(8,128)(2,1)}, u32[]{:S(2)}) copy-start(bf16[1,192,4096]{2,1,0:T(8,128)(2,1)} %param.12) | copy-start | bytes 4718596
  51.9 37.9 %copy-start.3 = (bf16[4096,32]{0,1:T(8,128)(2,1)S(1)}, bf16[4096,32]{0,1:T(8,128)(2,1)}, u32[]{:S(2)}) copy-start(bf16[4096,32]{0,1:T(8,128)(2,1)} %param.9) | copy-start | bytes 786436
  131.8 27.7 %copy-start.6 = (bf16[256,512]{1,0:T(8,128)(2,1)S(1)}, bf16[256,512]{1,0:T(8,128)(2,1)}, u32[]{:S(2)}) copy-start(bf16[256,512]{1,0:T(8,128)(2,1)} %copy-done.5) | copy-start | bytes 786436
  131.8 41.1 %all-to-all-start.3 = ((bf16[256,8,256]{2,1,0:T(8,128)(2,1)}), bf16[256,8,256]{2,1,0:T(8,128)(2,1)}, u32[]{:S(2)}, u32[]{:S(2)}) async-start(bf16[256,8,256]{2,1,0:T(8,128)(2,1)} %bitcast.31), calls=%async_computation.3 | async-start | bytes 2097152 | tf_op jit(solution)/shard_map/all_to_all | solution.py:424
  141.4 3.3 %collective-permute-start = (bf16[16,256]{1,0:T(8,128)(2,1)S(1)}, bf16[16,256]{1,0:T(8,128)(2,1)S(1)}, u32[]{:S(2)}, u32[]{:S(2)}) collective-permute-start(bf16[16,256]{1,0:T(8,128)(2,1)S(1)} %get-tuple-element.37), channel_id=1, source_target_pairs={{0,1},{1,0},{2,3},{3,2},{4,5},{5,4},{6,7},{7,6},{8,9},{9,8},{10,11... | collective-permute-start | bytes 24584 | tf_op jit(solution)/shard_map/ppermute | solution.py:385
  144.7 4.2 %collective-permute-start.1 = (bf16[32,256]{1,0:T(8,128)(2,1)S(1)}, bf16[32,256]{1,0:T(8,128)(2,1)S(1)}, u32[]{:S(2)}, u32[]{:S(2)}) collective-permute-start(bf16[32,256]{1,0:T(8,128)(2,1)S(1)} %maximum_select_fusion.1), channel_id=1, source_target_pairs={{0,8},{1,9},{2,10},{3,11},{4,12},{5,13},{6,14},{7,15},{8,16},{9,17... | collective-permute-start | bytes 49160 | tf_op jit(solution)/shard_map/ppermute | solution.py:385
  144.7 4.8 %collective-permute-start.2 = (bf16[32,256]{1,0:T(8,128)(2,1)S(1)}, bf16[32,256]{1,0:T(8,128)(2,1)S(1)}, u32[]{:S(2)}, u32[]{:S(2)}) collective-permute-start(bf16[32,256]{1,0:T(8,128)(2,1)S(1)} %maximum_select_fusion.1), channel_id=1, source_target_pairs={{0,16},{1,17},{2,18},{3,19},{4,20},{5,21},{6,22},{7,23},{8,24},{9,... | collective-permute-start | bytes 49160 | tf_op jit(solution)/shard_map/ppermute | solution.py:385
  146.5 3.3 %collective-permute-start.3 = (bf16[32,256]{1,0:T(8,128)(2,1)S(1)}, bf16[32,256]{1,0:T(8,128)(2,1)S(1)}, u32[]{:S(2)}, u32[]{:S(2)}) collective-permute-start(bf16[32,256]{1,0:T(8,128)(2,1)S(1)} %maximum_select_fusion.1), channel_id=1, source_target_pairs={{0,24},{1,25},{2,26},{3,27},{4,28},{5,29},{6,30},{7,31},{8,0},{9,1... | collective-permute-start | bytes 49160 | tf_op jit(solution)/shard_map/ppermute | solution.py:385
  149.8 17.9 %collective-permute-start.4 = (bf16[128,128]{1,0:T(8,128)(2,1)S(1)}, bf16[128,128]{1,0:T(8,128)(2,1)S(1)}, u32[]{:S(2)}, u32[]{:S(2)}) collective-permute-start(bf16[128,128]{1,0:T(8,128)(2,1)S(1)} %slice_select_fusion), channel_id=1, source_target_pairs={{0,2},{1,3},{2,4},{3,5},{4,6},{5,7},{6,0},{7,1},{8,10},{9,11},{10,... | collective-permute-start | bytes 98312 | tf_op jit(solution)/shard_map/ppermute | solution.py:385
  152.2 19.0 %collective-permute-start.5 = (bf16[128,128]{1,0:T(8,128)(2,1)S(1)}, bf16[128,128]{1,0:T(8,128)(2,1)S(1)}, u32[]{:S(2)}, u32[]{:S(2)}) collective-permute-start(bf16[128,128]{1,0:T(8,128)(2,1)S(1)} %slice_select_fusion), channel_id=1, source_target_pairs={{0,4},{1,5},{2,6},{3,7},{4,0},{5,1},{6,2},{7,3},{8,12},{9,13},{10,... | collective-permute-start | bytes 98312 | tf_op jit(solution)/shard_map/ppermute | solution.py:385
  156.7 14.5 %collective-permute-start.6 = (bf16[128,128]{1,0:T(8,128)(2,1)S(1)}, bf16[128,128]{1,0:T(8,128)(2,1)S(1)}, u32[]{:S(2)}, u32[]{:S(2)}) collective-permute-start(bf16[128,128]{1,0:T(8,128)(2,1)S(1)} %slice_select_fusion), channel_id=1, source_target_pairs={{0,6},{1,7},{2,0},{3,1},{4,2},{5,3},{6,4},{7,5},{8,14},{9,15},{10,... | collective-permute-start | bytes 98312 | tf_op jit(solution)/shard_map/ppermute | solution.py:385
  159.5 1.1 copy-start.4
  171.3 1.6 collective-permute-start.7
